TPU v7x, 512 devices: a whole 4x4x16 slice. The times are simulated.
512 devices in a mesh: dp: 32 (over x, y, core), expert: 16 (over z).
Axes of the slice: x: 4, y: 4, z: 16, core: 2. Of those that a mesh axis runs over, the one named last changes fastest.
Arguments:
- tokens: bfloat16 [65536, 2048], P(('dp', 'expert')), may hold values from -24 to 24
- cotangent: bfloat16 [65536, 2048], P(('dp', 'expert')), may hold values from -6 to 6
- expert_ids: int32 [65536, 8], P(('dp', 'expert')), may hold values from 0 to 127, as said below
- drop_mask: int32 [65536, 8], P(('dp', 'expert')), may hold values 0 or 1
- gate_table: float32 [65536, 8], P(('dp', 'expert')), may hold values from 0.1 to 1
- gate_weight: bfloat16 [2048, 3072], P('dp', 'expert'), may hold values from -0.125 to 0.125
- up_weight: bfloat16 [2048, 3072], P('dp', 'expert'), may hold values from -0.125 to 0.125
- down_weight: bfloat16 [3072, 2048], P('expert', 'dp'), may hold values from -0.21875 to 0.21875
Outputs:
- grad_tokens: bfloat16 [65536, 2048], P(('dp', 'expert'))
- grad_gate: float32 [2048, 3072], P('dp', 'expert')
- grad_up: float32 [2048, 3072], P('dp', 'expert')
- grad_down: float32 [3072, 2048], P('expert', 'dp')
Inputs may be any that keep to these rules, and one draw needn't show every extreme that they name: `expert_ids`: each row names 8 different experts.
All inputs are finite; a program needn't handle non-finite values. No bound on the sum of `drop_mask` on one device may be relied on, other than what follows from the above.
Results may differ from a plain program's by a relative error of at most 0.018.
Values may be sent and summed in bfloat16 or wider, within the bound.
A program may use at most 64 MiB of HBM per device.

v0:
```python
import jax
import jax.numpy as jnp
from jax import lax
from jax.sharding import PartitionSpec as P

SPLIT = 4
CAP = 16


def silu_parts(pre_gate):
    sigmoid_value = jax.nn.sigmoid(pre_gate)
    return (pre_gate * sigmoid_value, sigmoid_value * (1.0 + pre_gate * (1.0 - sigmoid_value)))


def slot_table(expert_ids, drop_mask, block_rows, in_flight):
    window = jnp.arange(in_flight, dtype=jnp.int32)
    hit_table = (
        (expert_ids[:, :, None] == window[None, None, :]) & (drop_mask[:, :, None] == 1)
    ).astype(jnp.int32)
    per_token = jnp.sum(hit_table, axis=1)
    blocked = per_token.reshape(-1, block_rows, in_flight)
    earlier = (jnp.cumsum(blocked, axis=1) - blocked).reshape(-1, in_flight)
    slot_rank = jnp.sum(hit_table * earlier[:, None, :], axis=2)
    is_live = (jnp.sum(hit_table, axis=2) > 0) & (slot_rank < CAP)
    return jnp.where(is_live, expert_ids * CAP + slot_rank, in_flight * CAP)


def body(tokens, cotangent, expert_ids, drop_mask, gate_table, gate_weight, up_weight, down_weight):
    expert_count = lax.axis_size("expert")
    in_flight = expert_count // SPLIT
    row_count = tokens.shape[0]
    model_width = tokens.shape[1]
    per_device = in_flight * CAP
    hidden = gate_weight.shape[1]
    contract_last = (((1,), (1,)), ((), ()))
    contract_first = (((0,), (0,)), ((), ()))
    local = slot_table(expert_ids, drop_mask, row_count, in_flight).reshape(-1)
    token_of = jnp.broadcast_to(
        jnp.arange(row_count, dtype=jnp.int32)[:, None], expert_ids.shape
    ).reshape(-1)
    slot_token = jnp.zeros((per_device,), jnp.int32).at[local].set(token_of, mode="drop")
    slot_gate = (
        jnp.zeros((per_device,), jnp.float32).at[local].set(gate_table.reshape(-1), mode="drop")
    )
    filled = jnp.zeros((per_device,), jnp.float32).at[local].set(1.0, mode="drop")
    own_in = jnp.where(filled[:, None] > 0, tokens[slot_token], jnp.zeros((), tokens.dtype))
    own_grad = (slot_gate[:, None] * cotangent[slot_token].astype(jnp.float32)).astype(jnp.bfloat16)

    def spread(values):
        widened = jnp.broadcast_to(
            values.reshape(in_flight, 1, CAP, model_width), (in_flight, SPLIT, CAP, model_width)
        )
        return widened.reshape(expert_count, CAP, model_width)

    arrived_in, arrived_grad = (
        lax.all_to_all(spread(own_in), "expert", split_axis=0, concat_axis=0, tiled=True),
        lax.all_to_all(spread(own_grad), "expert", split_axis=0, concat_axis=0, tiled=True),
    )
    rows_in = arrived_in.reshape(-1, model_width)
    rows_grad = arrived_grad.reshape(-1, model_width)
    stacked = jnp.concatenate([gate_weight, up_weight], axis=1)
    columns = rows_in
    pre_both = jnp.dot(
        columns,
        lax.all_gather(stacked, "dp", axis=0, tiled=True),
        preferred_element_type=jnp.float32,
    )
    columns = rows_grad
    grad_act = lax.dot_general(
        columns,
        lax.all_gather(down_weight, "dp", axis=1, tiled=True),
        contract_last,
        preferred_element_type=jnp.float32,
    )
    pre_gate = pre_both[:, :hidden]
    pre_up = pre_both[:, hidden:]
    silu_value, silu_slope = silu_parts(pre_gate)
    activated = (silu_value * pre_up).astype(jnp.bfloat16)
    grad_gate_pre = (grad_act * pre_up * silu_slope).astype(jnp.bfloat16)
    grad_up_pre = (grad_act * silu_value).astype(jnp.bfloat16)
    grad_pair = jnp.concatenate([grad_gate_pre, grad_up_pre], axis=1)
    slot_grad = lax.dot_general(
        grad_pair,
        lax.all_gather(stacked, "dp", axis=0, tiled=True),
        contract_last,
        preferred_element_type=jnp.float32,
    )
    slot_part = slot_grad.astype(jnp.bfloat16).reshape(expert_count, CAP, model_width)
    returned = lax.all_to_all(slot_part, "expert", split_axis=0, concat_axis=0, tiled=True)
    per_slot = jnp.sum(
        returned.astype(jnp.float32).reshape(in_flight, SPLIT, CAP, model_width), axis=1
    ).reshape(per_device, model_width)
    grad_tokens = (
        jnp.zeros((row_count, model_width), jnp.float32)
        .at[slot_token]
        .add(per_slot * filled[:, None])
    )
    pair_term = lax.dot_general(
        rows_in, grad_pair, contract_first, preferred_element_type=jnp.float32
    )
    down_term = lax.dot_general(
        rows_grad, activated, contract_first, preferred_element_type=jnp.float32
    )
    summed = lax.psum_scatter(
        jnp.concatenate([pair_term, down_term], axis=1).astype(jnp.bfloat16),
        "dp",
        scatter_dimension=0,
        tiled=True,
    ).astype(jnp.float32)
    return (
        grad_tokens.astype(jnp.bfloat16),
        summed[:, :hidden],
        summed[:, hidden : 2 * hidden],
        summed[:, 2 * hidden :].T,
    )


def solution(mesh):
    return jax.shard_map(
        body,
        mesh=mesh,
        in_specs=(
            P(("dp", "expert"), None),
            P(("dp", "expert"), None),
            P(("dp", "expert"), None),
            P(("dp", "expert"), None),
            P(("dp", "expert"), None),
            P("dp", "expert"),
            P("dp", "expert"),
            P("expert", "dp"),
        ),
        out_specs=(
            P(("dp", "expert"), None),
            P("dp", "expert"),
            P("dp", "expert"),
            P("expert", "dp"),
        ),
        check_vma=False,
    )
```

profile of v0, /device:TPU:24, one launch (start us, length us, event | category | flops | bytes accessed | tf_op | source)
XLA Modules:
  0.0 282.3 jit_solution(8985810166808604248)
XLA Ops:
  7.2 0.0 copy-start
  7.2 0.7 broadcast_compare_fusion
  7.9 0.7 convert_reduce_fusion.2
  8.6 0.1 copy.37
  8.8 0.2 reduce_window_sum.11
  8.9 0.1 copy.39
  9.0 0.7 select_reduce_fusion
  9.7 0.7 add_select_fusion
  10.4 0.1 copy.40
  10.5 0.1 reshape.120
  10.6 0.1 reshape.154
  10.7 4.3 %scatter_custom_fusion = s32[64]{0:T(128)S(1)} fusion(s32[1024]{0:T(1024)S(1)} %bitcast.30, s32[1024]{0:T(1024)S(1)} %reshape.154, s32[]{:T(128)} %constant.9.clone.1), kind=kCustom, calls=%fused_computation.40 | custom fusion | bytes 260 | tf_op jit(solution)/shard_map/scatter | solution.py:41
  15.1 4.3 %scatter_custom_fusion.2 = f32[64]{0:T(128)S(1)} fusion(s32[1024]{0:T(1024)S(1)} %bitcast.31, f32[1024]{0:T(1024)S(1)} %broadcast.67, f32[]{:T(128)} %constant.8.clone.1), kind=kCustom, calls=%fused_computation.36 | custom fusion | bytes 260 | tf_op jit(solution)/shard_map/scatter | solution.py:45
  19.4 0.1 broadcast_in_dim.60
  19.5 0.0 copy-done
  19.5 0.7 gather_fusion.1
  20.2 0.0 copy-start.1
  20.2 0.1 broadcast_select_fusion
  20.3 1.1 broadcast_in_dim.63
  21.5 0.0 copy-start.6
  21.5 15.3 %all-to-all-start.1 = ((bf16[16,16,2048]{2,1,0:T(8,128)(2,1)}), bf16[16,16,2048]{2,1,0:T(8,128)(2,1)S(1)}, u32[]{:S(2)}, u32[]{:S(2)}) async-start(bf16[16,16,2048]{2,1,0:T(8,128)(2,1)} %bitcast.5), calls=%async_computation.1 | async-start | bytes 2097152 | tf_op jit(solution)/shard_map/all_to_all | solution.py:56
  36.8 0.0 copy-done.1
  36.8 0.7 gather_fusion
  37.5 0.0 copy-done.6
  37.6 0.0 copy-start.3
  37.6 0.0 copy-start.4
  37.6 0.1 copy.41
  37.7 0.1 reshape.162
  37.8 4.3 %scatter_custom_fusion.1 = f32[64]{0:T(128)S(1)} fusion(s32[1024]{0:T(1024)S(1)} %bitcast.32, f32[1024]{0:T(1024)S(1)} %reshape.162, f32[]{:T(128)} %constant.8.clone.1), kind=kCustom, calls=%fused_computation.38 | custom fusion | bytes 260 | tf_op jit(solution)/shard_map/scatter | solution.py:43
  42.1 0.1 mul.57
  42.2 0.1 fusion
  42.3 44.5 %all-to-all-done.1 = bf16[16,16,2048]{2,1,0:T(8,128)(2,1)S(1)} async-done(((bf16[16,16,2048]{2,1,0:T(8,128)(2,1)}), bf16[16,16,2048]{2,1,0:T(8,128)(2,1)S(1)}, u32[]{:S(2)}, u32[]{:S(2)}) %all-to-all-start.1) | async-done | bytes 1048608 | tf_op jit(solution)/shard_map/all_to_all | solution.py:56
  86.8 1.1 broadcast_in_dim.58
  87.9 7.9 %all-to-all-start = ((bf16[16,16,2048]{2,1,0:T(8,128)(2,1)}), bf16[16,16,2048]{2,1,0:T(8,128)(2,1)S(1)}, u32[]{:S(2)}, u32[]{:S(2)}) async-start(bf16[16,16,2048]{2,1,0:T(8,128)(2,1)} %bitcast.2), calls=%async_computation | async-start | bytes 2097152 | tf_op jit(solution)/shard_map/all_to_all | solution.py:57
  95.8 0.0 all-gather.2.cloned.1.call-start
  95.8 0.0 copy-done.3
  95.8 0.0 copy-done.4
  95.8 0.7 pad_maximum_fusion.4
  96.5 0.0 all-gather.2.cloned.1.call-update
  96.6 0.0 reduce-scatter.4.cloned.1.call-start
  96.6 0.0 copy-done.5
  96.6 27.0 %all_gather.7 = bf16[192,2048]{0,1:T(8,128)(2,1)} all-gather(bf16[192,64]{0,1:T(8,128)(2,1)S(1)} %copy-done.5), channel_id=1, replica_groups=mesh['dp'=32,'expert'=16] {'dp'}, dimensions={1}, use_global_device_ids=true | all-gather | bytes 811008 | tf_op jit(solution)/shard_map/all_gather | solution.py:71
  123.6 35.9 %all-gather.2.cloned.1.call-done = bf16[2048,384]{1,0:T(8,128)(2,1)} async-done(((bf16[64,384]{1,0:T(8,128)(2,1)}), bf16[2048,384]{1,0:T(8,128)(2,1)}) %all-gather.2.cloned.1.call-update) | async-done | bytes 1572880 | tf_op jit(solution)/shard_map/all_gather | solution.py:65
  159.5 2.1 fusion.16
  161.7 0.0 all-to-all-done
  161.7 0.4 convolution_convert_fusion.2
  162.1 1.8 multiply_convert_fusion.2
  163.9 0.6 convolution_convert_fusion
  164.5 0.3 pad_maximum_fusion
  164.7 2.6 copy.48
  167.3 0.0 reduce-scatter.4.cloned.1.call-update
  167.4 1.4 copy-done.2
  168.7 1.7 convolution_convert_fusion.1
  170.5 12.3 %all-to-all-start.2 = ((bf16[16,16,2048]{2,1,0:T(8,128)(2,1)}), bf16[16,16,2048]{2,1,0:T(8,128)(2,1)S(1)}, u32[]{:S(2)}, u32[]{:S(2)}) async-start(bf16[16,16,2048]{2,1,0:T(8,128)(2,1)} %bitcast.7), calls=%async_computation.2 | async-start | bytes 2097152 | tf_op jit(solution)/shard_map/all_to_all | solution.py:89
  182.8 86.7 %reduce-scatter.4.cloned.1.call-done = bf16[64,576]{1,0:T(8,128)(2,1)} async-done(((bf16[2048,576]{1,0:T(8,128)(2,1)}), bf16[64,576]{1,0:T(8,128)(2,1)}) %reduce-scatter.4.cloned.1.call-update) | async-done | bytes 73744
  269.4 1.0 copy.49
  270.5 0.7 copy.44
  271.2 0.7 copy.45
  272.0 0.7 copy.46
  272.7 0.0 all-to-all-done.2
  272.7 0.2 convert_reduce_fusion
  272.8 0.1 bitcast_multiply_fusion
  273.0 1.6 scatter_custom_fusion.3
  274.6 0.9 convert_element_type.47
  (12 shorter events, 0.1 us)
Async XLA Ops:
  7.2 12.3 %copy-start = (bf16[128,2048]{1,0:T(8,128)(2,1)S(1)}, bf16[128,2048]{1,0:T(8,128)(2,1)}, u32[]{:S(2)}) copy-start(bf16[128,2048]{1,0:T(8,128)(2,1)} %param.8) | copy-start | bytes 1572868
  20.2 16.6 %copy-start.1 = (bf16[128,2048]{1,0:T(8,128)(2,1)S(1)}, bf16[128,2048]{1,0:T(8,128)(2,1)}, u32[]{:S(2)}) copy-start(bf16[128,2048]{1,0:T(8,128)(2,1)} %param.9) | copy-start | bytes 1572868
  21.5 16.1 %copy-start.6 = (f32[128,8]{0,1:T(8,128)S(1)}, f32[128,8]{0,1:T(8,128)}, u32[]{:S(2)}) copy-start(f32[128,8]{0,1:T(8,128)} %param.12) | copy-start | bytes 12292
  21.5 65.3 %all-to-all-start.1 = ((bf16[16,16,2048]{2,1,0:T(8,128)(2,1)}), bf16[16,16,2048]{2,1,0:T(8,128)(2,1)S(1)}, u32[]{:S(2)}, u32[]{:S(2)}) async-start(bf16[16,16,2048]{2,1,0:T(8,128)(2,1)} %bitcast.5), calls=%async_computation.1 | async-start | bytes 2097152 | tf_op jit(solution)/shard_map/all_to_all | solution.py:56
  37.6 58.3 %copy-start.3 = (bf16[64,192]{1,0:T(8,128)(2,1)S(1)}, bf16[64,192]{1,0:T(8,128)(2,1)}, u32[]{:S(2)}) copy-start(bf16[64,192]{1,0:T(8,128)(2,1)} %param.14) | copy-start | bytes 73732
  37.6 58.3 %copy-start.4 = (bf16[64,192]{1,0:T(8,128)(2,1)S(1)}, bf16[64,192]{1,0:T(8,128)(2,1)}, u32[]{:S(2)}) copy-start(bf16[64,192]{1,0:T(8,128)(2,1)} %param.13) | copy-start | bytes 73732
  37.7 58.9 %copy-start.5 = (bf16[192,64]{0,1:T(8,128)(2,1)S(1)}, bf16[192,64]{0,1:T(8,128)(2,1)}, u32[]{:S(2)}) copy-start(bf16[192,64]{0,1:T(8,128)(2,1)} %param.15) | copy-start | bytes 73732
  87.9 73.8 %all-to-all-start = ((bf16[16,16,2048]{2,1,0:T(8,128)(2,1)}), bf16[16,16,2048]{2,1,0:T(8,128)(2,1)S(1)}, u32[]{:S(2)}, u32[]{:S(2)}) async-start(bf16[16,16,2048]{2,1,0:T(8,128)(2,1)} %bitcast.2), calls=%async_computation | async-start | bytes 2097152 | tf_op jit(solution)/shard_map/all_to_all | solution.py:57
  95.8 63.8 %all-gather.2.cloned.1.call-start = ((), (), s32[]{:S(2)}) async-start(), calls=%async_computation.4 | async-start | bytes 1622016 | tf_op jit(solution)/shard_map/all_gather | solution.py:65
  96.6 172.9 %reduce-scatter.4.cloned.1.call-start = ((), (), s32[]{:S(2)}) async-start(), calls=%async_computation.5 | async-start | bytes 2703360
  167.3 1.4 copy-start.2
  170.5 102.2 %all-to-all-start.2 = ((bf16[16,16,2048]{2,1,0:T(8,128)(2,1)}), bf16[16,16,2048]{2,1,0:T(8,128)(2,1)S(1)}, u32[]{:S(2)}, u32[]{:S(2)}) async-start(bf16[16,16,2048]{2,1,0:T(8,128)(2,1)} %bitcast.7), calls=%async_computation.2 | async-start | bytes 2097152 | tf_op jit(solution)/shard_map/all_to_all | solution.py:89
Sparse Core Ops, SparseCore 0:
  100.3 59.1 all-gather.1
  167.5 101.9 reduce-scatter.3
where the time goes:
time: 283 us; the launch traced here: 282 us
  waiting for transfers between devices  167 us (59%)
  starting transfers between devices  35.6 us (13%)
  blocking collectives  27 us (10%)
  local copies, waits for them, and re-layouts  24.6 us (9%)
  between operations  14.3 us (5%)
  other arithmetic  7.02 us (2%)
  matrix products  6.63 us (2%)
    unnamed x3, waiting for transfers between devices  86.7 us
    all_to_all x1, waiting for transfers between devices, body(): lax.all_to_all(spread(own_in), 'expert', split_axis=0, concat_axis=0, til...  44.5 us
    all_gather x1, waiting for transfers between devices, body(): lax.all_gather(stacked, 'dp', axis=0, tiled=True)  35.9 us
    all_gather x1, blocking collectives, body(): lax.all_gather(down_weight, 'dp', axis=1, tiled=True)  27 us
    all_to_all x1, starting transfers between devices, body(): lax.all_to_all(spread(own_in), 'expert', split_axis=0, concat_axis=0, til...  15.3 us
    all_to_all x1, starting transfers between devices, body(): lax.all_to_all(slot_part, 'expert', split_axis=0, concat_axis=0, tiled=True)  12.3 us
    all_to_all x1, starting transfers between devices, body(): lax.all_to_all(spread(own_grad), 'expert', split_axis=0, concat_axis=0, t...  7.88 us
    unnamed x20, local copies, waits for them, and re-layouts  7.26 us
  transfers between devices with their start and end apart: 5, of which 3 were waited for; matrix products, arithmetic and copies ran while one was open for 5% of the time, Pallas kernels for 0%

commit v1 on v0

v1 whole, which is shorter than its diff:
```python
import functools

import jax
import jax.numpy as jnp
from jax import lax
from jax.experimental import pallas as pl
from jax.experimental.pallas import tpu as pltpu
from jax.sharding import PartitionSpec as P

MESH = pl.DeviceIdType.MESH
RING = 16
SPLIT = 4
CAP = 16
FAR = SPLIT + 2
REACH = FAR + SPLIT - 1
LAST = (((1,), (1,)), ((), ()))
FIRST = (((0,), (0,)), ((), ()))


def copy_to(src, dst, send_sem, recv_sem, device):
    return pltpu.make_async_remote_copy(
        src_ref=src,
        dst_ref=dst,
        send_sem=send_sem,
        recv_sem=recv_sem,
        device_id=device,
        device_id_type=MESH,
    )


def kernel(
    tokens,
    cotangent,
    ids,
    mask,
    gates,
    gate_w,
    up_w,
    down_w,
    grad_tokens,
    grad_gate,
    grad_up,
    grad_down,
    place,
    out_in,
    out_grad,
    rows_in,
    rows_grad,
    weights,
    pre,
    act,
    pair,
    active,
    parts,
    from_right,
    from_left,
    finals,
    grads,
    sibling_grads,
    grads_in,
    direct_send,
    pass_right,
    pass_left,
    rows_recv,
    weight_send,
    weight_recv,
    back_left,
    back_right,
    right_recv,
    left_recv,
    final_recv,
    sibling_send,
    sibling_recv,
    grad_send,
    grad_recv,
):
    width = tokens.shape[1]
    hidden = gate_w.shape[1]
    depth = gate_w.shape[0]
    n_dp = weights.shape[0]
    half = n_dp // 2
    n_tok = tokens.shape[0]
    n_rows = RING * CAP
    step = min(256, width // 2)
    blocks = step // depth
    lanes = weights.shape[2]

    dp = lax.axis_index("dp")
    z = lax.axis_index("expert")
    group = z // SPLIT
    member = lax.rem(z, SPLIT)
    core = lax.rem(dp, 2)
    chip = dp // 2
    sibling = dp + 1 - 2 * core

    def plane(offset):
        return (dp, lax.rem(z + offset + RING, RING))

    barrier = pltpu.get_barrier_semaphore()

    def greet_ring(i, carry):
        pl.semaphore_signal(barrier, inc=1, device_id=plane(i), device_id_type=MESH)
        return carry

    def greet_plane(i, carry):
        pl.semaphore_signal(
            barrier, inc=1, device_id=(lax.rem(dp + i, n_dp), z), device_id_type=MESH
        )
        return carry

    lax.fori_loop(1, RING, greet_ring, 0)
    lax.fori_loop(1, n_dp, greet_plane, 0)

    live = mask[...] == 1
    hits, gate_rows = [], []
    for j in range(SPLIT):
        hit = jnp.where((ids[...] == j) & live, 1.0, 0.0)
        hits.append(jnp.sum(hit, axis=0, keepdims=True))
        gate_rows.append(jnp.sum(hit * gates[...], axis=0, keepdims=True))
    hit_rows = jnp.concatenate(hits + [jnp.zeros((CAP - SPLIT, n_tok), jnp.float32)], axis=0)
    earlier = (
        lax.broadcasted_iota(jnp.int32, (n_tok, n_tok), 0)
        < lax.broadcasted_iota(jnp.int32, (n_tok, n_tok), 1)
    )
    rank = jnp.dot(
        hit_rows.astype(jnp.bfloat16),
        jnp.where(earlier, 1.0, 0.0).astype(jnp.bfloat16),
        preferred_element_type=jnp.float32,
    )
    slot = lax.broadcasted_iota(jnp.int32, (CAP, n_tok), 0).astype(jnp.float32)
    slot_gates = []
    for j in range(SPLIT):
        held = jnp.where(
            (jnp.broadcast_to(rank[j : j + 1], (CAP, n_tok)) == slot)
            & (jnp.broadcast_to(hits[j], (CAP, n_tok)) > 0.5),
            1.0,
            0.0,
        )
        place[j] = held.astype(jnp.bfloat16)
        slot_gates.append(jnp.sum(held * gate_rows[j], axis=1, keepdims=True))
    slot_gate = jnp.concatenate(slot_gates, axis=0)
    chosen = place[...].reshape(SPLIT * CAP, n_tok)

    def fill(c, carry):
        cols = pl.ds(pl.multiple_of(c * step, step), step)
        picked = jnp.dot(chosen, tokens[:, cols], preferred_element_type=jnp.float32)
        out_in[:, :, cols] = picked.astype(jnp.bfloat16).reshape(SPLIT, CAP, step)
        picked = jnp.dot(chosen, cotangent[:, cols], preferred_element_type=jnp.float32)
        out_grad[:, :, cols] = (
            (slot_gate * picked).astype(jnp.bfloat16).reshape(SPLIT, CAP, step)
        )
        return carry

    lax.fori_loop(0, width // step, fill, 0)

    packed = jnp.concatenate(
        [
            gate_w[...].astype(jnp.float32),
            up_w[...].astype(jnp.float32),
            down_w[...].astype(jnp.float32),
            jnp.zeros((depth, lanes - 3 * hidden), jnp.float32),
        ],
        axis=1,
    )
    weights[dp] = packed.astype(jnp.bfloat16)

    pl.semaphore_wait(barrier, RING - 1 + n_dp - 1)

    upper = member // 2
    both = ((out_in, rows_in), (out_grad, rows_grad))

    def direct(index, offset, slot_there, expert):
        for h, (source, rows) in enumerate(both):
            yield copy_to(
                source.at[expert],
                rows.at[slot_there],
                direct_send.at[index, h],
                rows_recv.at[slot_there, h],
                plane(offset),
            )

    far = list(
        direct(
            0,
            upper * (8 - member) - (1 - upper) * (member + 5),
            upper * (8 + member) + (1 - upper) * (member + 5),
            lax.rem(group + 2, SPLIT),
        )
    )
    near = list(direct(1, 4 - member, 12 + member, lax.rem(group + 1, SPLIT)))
    near += list(direct(2, -(member + 1), member + 1, lax.rem(group + 3, SPLIT)))
    own_right = list(direct(3, 1, RING - 1, group))
    own_left = list(direct(4, -1, 1, group))

    @pl.when(member < SPLIT - 1)
    def _():
        for copy in own_right:
            copy.start()

    @pl.when(member > 0)
    def _():
        for copy in own_left:
            copy.start()

    for copy in near + far:
        copy.start()

    def weight_copy(i):
        return copy_to(
            weights.at[dp],
            weights.at[dp],
            weight_send.at[i],
            weight_recv.at[dp],
            (lax.rem(dp + i, n_dp), z),
        )

    def send_weights(i, carry):
        weight_copy(i).start()
        return carry

    lax.fori_loop(1, n_dp, send_weights, 0)

    rows_in[0] = out_in[group]
    rows_grad[0] = out_grad[group]

    def right_pass(k, h, rows):
        return copy_to(
            rows.at[RING - k],
            rows.at[RING - k - 1],
            pass_right.at[k, h],
            rows_recv.at[RING - k - 1, h],
            plane(1),
        )

    def left_pass(k, h, rows):
        return copy_to(
            rows.at[k],
            rows.at[k + 1],
            pass_left.at[k, h],
            rows_recv.at[k + 1, h],
            plane(-1),
        )

    def arrived(slot_here, h, rows):
        copy_to(
            rows.at[slot_here],
            rows.at[slot_here],
            direct_send.at[0, h],
            rows_recv.at[slot_here, h],
            plane(1),
        ).wait_recv()

    def pass_rows(k, carry):
        @pl.when(k <= member + FAR)
        def _():
            for h, (_, rows) in enumerate(both):
                arrived(RING - k, h, rows)

                @pl.when(member < SPLIT - 1)
                def _():
                    right_pass(k, h, rows).start()

        @pl.when(k <= REACH - member)
        def _():
            for h, (_, rows) in enumerate(both):
                arrived(k, h, rows)

                @pl.when(member > 0)
                def _():
                    left_pass(k, h, rows).start()

        return carry

    lax.fori_loop(1, REACH + 1, pass_rows, 0)

    def weights_arrived(i, carry):
        source = lax.rem(dp + i, n_dp)
        copy_to(
            weights.at[source],
            weights.at[source],
            weight_send.at[i],
            weight_recv.at[source],
            (sibling, z),
        ).wait_recv()
        return carry

    lax.fori_loop(1, n_dp, weights_arrived, 0)

    pre[...] = jnp.zeros_like(pre)
    act[...] = jnp.zeros_like(act)

    def project(c, carry):
        cols = pl.ds(pl.multiple_of(c * step, step), step)
        block = weights[pl.ds(c * blocks, blocks)].reshape(step, lanes)
        left = rows_in[:, :, cols].reshape(n_rows, step)
        pre[...] += jnp.dot(left, block[:, : 2 * hidden], preferred_element_type=jnp.float32)
        left = rows_grad[:, :, cols].reshape(n_rows, step)
        act[...] += jnp.dot(left, block[:, 2 * hidden :], preferred_element_type=jnp.float32)
        return carry

    lax.fori_loop(0, width // step, project, 0)

    pre_gate = pre[:, :hidden]
    pre_up = pre[:, hidden:]
    grad_act = act[:, :hidden]
    sigmoid_value = jax.nn.sigmoid(pre_gate)
    silu_value = pre_gate * sigmoid_value
    slope = sigmoid_value * (1.0 + pre_gate * (1.0 - sigmoid_value))
    pair[...] = jnp.concatenate(
        [grad_act * pre_up * slope, grad_act * silu_value], axis=1
    ).astype(jnp.bfloat16)
    active[...] = jnp.concatenate(
        [silu_value * pre_up, jnp.zeros((n_rows, act.shape[1] - hidden), jnp.float32)], axis=1
    ).astype(jnp.bfloat16)

    def back_project(c, carry):
        cols = pl.ds(pl.multiple_of(c * step, step), step)
        block = weights[pl.ds(c * blocks, blocks)].reshape(step, lanes)
        part = lax.dot_general(
            pair[...], block[:, : 2 * hidden], LAST, preferred_element_type=jnp.float32
        )
        parts[:, :, cols] = part.astype(jnp.bfloat16).reshape(RING, CAP, step)
        return carry

    lax.fori_loop(0, width // step, back_project, 0)

    def left_chain(k):
        return copy_to(
            parts.at[RING - k],
            from_right.at[k - 1],
            back_left.at[k],
            right_recv.at[k - 1],
            plane(-1),
        )

    def left_exit(k):
        to = k // 5
        return copy_to(
            parts.at[RING - k],
            finals.at[to],
            back_left.at[k],
            final_recv.at[to],
            plane(-k),
        )

    def right_chain(k):
        return copy_to(
            parts.at[k],
            from_left.at[k - 1],
            back_right.at[k],
            left_recv.at[k - 1],
            plane(1),
        )

    def right_exit(k):
        to = 2 - k // 5
        return copy_to(
            parts.at[k],
            finals.at[to],
            back_right.at[k],
            final_recv.at[to],
            plane(k),
        )

    def got_right(k):
        copy_to(
            from_right.at[k], from_right.at[k], back_left.at[0], right_recv.at[k], plane(1)
        ).wait_recv()

    def got_left(k):
        copy_to(
            from_left.at[k], from_left.at[k], back_right.at[0], left_recv.at[k], plane(-1)
        ).wait_recv()

    def add_bf16(one, two):
        return (one.astype(jnp.float32) + two.astype(jnp.float32)).astype(jnp.bfloat16)

    @pl.when(member == SPLIT - 1)
    def _():
        def start(i, carry):
            left_chain(REACH - i).start()
            return carry

        lax.fori_loop(0, REACH, start, 0)

    @pl.when(member == 0)
    def _():
        def start(i, carry):
            right_chain(REACH - i).start()
            return carry

        lax.fori_loop(0, REACH, start, 0)

    def weight_grads(c, carry):
        first = lax.rem(c * blocks + (1 - core) * half, n_dp)
        cols = pl.ds(pl.multiple_of(first * depth, step), step)
        left = rows_in[:, :, cols].reshape(n_rows, step)
        one = lax.dot_general(left, pair[...], FIRST, preferred_element_type=jnp.float32)
        left = rows_grad[:, :, cols].reshape(n_rows, step)
        two = lax.dot_general(left, active[...], FIRST, preferred_element_type=jnp.float32)
        grads[pl.ds(first, blocks)] = (
            jnp.concatenate([one, two], axis=1).astype(jnp.bfloat16).reshape(blocks, depth, lanes)
        )
        return carry

    chunks = width // step
    lax.fori_loop(0, chunks // 2, weight_grads, 0)
    to_sibling = copy_to(
        grads.at[pl.ds((1 - core) * half, half)],
        sibling_grads,
        sibling_send,
        sibling_recv,
        (sibling, z),
    )
    to_sibling.start()
    lax.fori_loop(chunks // 2, chunks, weight_grads, 0)

    def pass_sums(i, carry):
        k = REACH - i

        @pl.when((k <= member + FAR) & (member < SPLIT - 1))
        def _():
            got_right(k)
            parts[RING - k] = add_bf16(parts[RING - k], from_right[k])

            @pl.when(member > 0)
            def _():
                left_chain(k).start()

            @pl.when(member == 0)
            def _():
                left_exit(k).start()

        @pl.when((k <= REACH - member) & (member > 0))
        def _():
            got_left(k)
            parts[k] = add_bf16(parts[k], from_left[k])

            @pl.when(member < SPLIT - 1)
            def _():
                right_chain(k).start()

            @pl.when(member == SPLIT - 1)
            def _():
                right_exit(k).start()

        return carry

    lax.fori_loop(0, REACH, pass_sums, 0)

    to_sibling.wait_recv()

    def grad_copy(i):
        return copy_to(
            grads.at[core * half + i],
            grads_in.at[chip],
            grad_send.at[i],
            grad_recv.at[chip],
            (core * half + i, z),
        )

    def send_grads(i, carry):
        to = core * half + i
        summed = add_bf16(grads[to], sibling_grads[i])
        grads[to] = summed

        @pl.when(to != dp)
        def _():
            grad_copy(i).start()

        @pl.when(to == dp)
        def _():
            grads_in[chip] = summed

        return carry

    lax.fori_loop(0, half, send_grads, 0)

    @pl.when(member < SPLIT - 1)
    def _():
        got_right(0)

    @pl.when(member == SPLIT - 1)
    def _():
        from_right[0] = jnp.zeros((CAP, width), jnp.bfloat16)

    @pl.when(member > 0)
    def _():
        got_left(0)

    @pl.when(member == 0)
    def _():
        from_left[0] = jnp.zeros((CAP, width), jnp.bfloat16)

    for i in range(3):
        copy_to(
            finals.at[i], finals.at[i], back_left.at[0], final_recv.at[i], plane(1)
        ).wait_recv()

    own_place = place[group]
    where_from = jnp.concatenate(
        [
            place[lax.rem(group + 1, SPLIT)],
            place[lax.rem(group + 2, SPLIT)],
            place[lax.rem(group + 3, SPLIT)],
            own_place,
            own_place,
            own_place,
        ],
        axis=0,
    )

    def give_back(c, carry):
        cols = pl.ds(pl.multiple_of(c * step, step), step)
        values = jnp.concatenate(
            [
                finals[:, :, cols].reshape(3 * CAP, step),
                parts[0, :, cols],
                from_right[0, :, cols],
                from_left[0, :, cols],
            ],
            axis=0,
        )
        grad_tokens[:, cols] = lax.dot_general(
            where_from, values, FIRST, preferred_element_type=jnp.float32
        ).astype(jnp.bfloat16)
        return carry

    lax.fori_loop(0, width // step, give_back, 0)

    def grads_arrived(i, carry):
        sender = 2 * i + dp // half

        @pl.when(sender != dp)
        def _():
            copy_to(
                grads_in.at[i], grads_in.at[i], grad_send.at[i], grad_recv.at[i], (sibling, z)
            ).wait_recv()

        return carry

    lax.fori_loop(0, half, grads_arrived, 0)
    total = jnp.sum(grads_in[...].astype(jnp.float32), axis=0)
    grad_gate[...] = total[:, :hidden]
    grad_up[...] = total[:, hidden : 2 * hidden]
    grad_down[...] = total[:, 2 * hidden : 3 * hidden]

    for copy in near + far:
        copy.wait_send()

    @pl.when(member < SPLIT - 1)
    def _():
        for copy in own_right:
            copy.wait_send()

    @pl.when(member > 0)
    def _():
        for copy in own_left:
            copy.wait_send()

    def drain(k, carry):
        @pl.when(k <= member + FAR)
        def _():
            left_chain(k).wait_send()

            @pl.when(member < SPLIT - 1)
            def _():
                for h, (_, rows) in enumerate(both):
                    right_pass(k, h, rows).wait_send()

        @pl.when(k <= REACH - member)
        def _():
            right_chain(k).wait_send()

            @pl.when(member > 0)
            def _():
                for h, (_, rows) in enumerate(both):
                    left_pass(k, h, rows).wait_send()

        return carry

    lax.fori_loop(1, REACH + 1, drain, 0)

    def drain_weights(i, carry):
        weight_copy(i).wait_send()
        return carry

    lax.fori_loop(1, n_dp, drain_weights, 0)
    to_sibling.wait_send()

    def drain_grads(i, carry):
        @pl.when(core * half + i != dp)
        def _():
            grad_copy(i).wait_send()

        return carry

    lax.fori_loop(0, half, drain_grads, 0)


def body(n_dp, tokens, cotangent, ids, mask, gates, gate_w, up_w, down_w):
    n_tok, width = tokens.shape
    depth, hidden = gate_w.shape
    lanes = -(-3 * hidden // 128) * 128
    n_rows = RING * CAP
    half = n_dp // 2
    bf16, f32 = jnp.bfloat16, jnp.float32
    vmem = pl.BlockSpec(memory_space=pltpu.VMEM)
    dma = pltpu.SemaphoreType.DMA
    grad_tokens, grad_gate, grad_up, grad_down = pl.pallas_call(
        kernel,
        out_shape=(
            jax.ShapeDtypeStruct((n_tok, width), bf16),
            jax.ShapeDtypeStruct((depth, hidden), f32),
            jax.ShapeDtypeStruct((depth, hidden), f32),
            jax.ShapeDtypeStruct((depth, hidden), f32),
        ),
        in_specs=[vmem] * 8,
        out_specs=[vmem] * 4,
        scratch_shapes=[
            pltpu.VMEM((SPLIT, CAP, n_tok), bf16),
            pltpu.VMEM((SPLIT, CAP, width), bf16),
            pltpu.VMEM((SPLIT, CAP, width), bf16),
            pltpu.VMEM((RING, CAP, width), bf16),
            pltpu.VMEM((RING, CAP, width), bf16),
            pltpu.VMEM((n_dp, depth, lanes), bf16),
            pltpu.VMEM((n_rows, 2 * hidden), f32),
            pltpu.VMEM((n_rows, lanes - 2 * hidden), f32),
            pltpu.VMEM((n_rows, 2 * hidden), bf16),
            pltpu.VMEM((n_rows, lanes - 2 * hidden), bf16),
            pltpu.VMEM((RING, CAP, width), bf16),
            pltpu.VMEM((REACH + 1, CAP, width), bf16),
            pltpu.VMEM((REACH + 1, CAP, width), bf16),
            pltpu.VMEM((3, CAP, width), bf16),
            pltpu.VMEM((n_dp, depth, lanes), bf16),
            pltpu.VMEM((half, depth, lanes), bf16),
            pltpu.VMEM((half, depth, lanes), bf16),
            dma((5, 2)),
            dma((REACH + 1, 2)),
            dma((REACH + 1, 2)),
            dma((RING, 2)),
            dma((n_dp,)),
            dma((n_dp,)),
            dma((REACH + 1,)),
            dma((REACH + 1,)),
            dma((REACH + 1,)),
            dma((REACH + 1,)),
            dma((3,)),
            dma,
            dma,
            dma((half,)),
            dma((half,)),
        ],
        compiler_params=pltpu.CompilerParams(
            collective_id=0, has_side_effects=True, vmem_limit_bytes=48 * 1024 * 1024
        ),
        cost_estimate=pl.CostEstimate(
            flops=16 * n_rows * width * hidden, bytes_accessed=1 << 21, transcendentals=1 << 16
        ),
    )(tokens, cotangent, ids.T, mask.T, gates.T, gate_w, up_w, down_w.T)
    return grad_tokens, grad_gate, grad_up, grad_down.T


def solution(mesh):
    rows = P(("dp", "expert"), None)
    return jax.shard_map(
        functools.partial(body, mesh.shape["dp"]),
        mesh=mesh,
        in_specs=(rows, rows, rows, rows, rows) + (P("dp", "expert"),) * 2 + (P("expert", "dp"),),
        out_specs=(rows, P("dp", "expert"), P("dp", "expert"), P("expert", "dp")),
        check_vma=False,
    )
```

time: 283 us -> 127 us (0.45)
  waiting for transfers between devices: 167 us -> 0 us
  Pallas kernels: 0 us -> 116 us
  starting transfers between devices: 35.6 us -> 0 us
  blocking collectives: 27 us -> 0 us
  local copies, waits for them, and re-layouts: 24.6 us -> 9.09 us
  between operations: 14.3 us -> 0.66 us
  other arithmetic: 7.02 us -> 0 us
  matrix products: 6.63 us -> 0 us
    pallas_call x0 -> x1, Pallas kernels: none -> 116 us  [body(): pl.pallas_call(kernel, out_shape=(jax.ShapeDtypeStruct((n_tok, width), bf...]
    unnamed x3 -> x0, waiting for transfers between devices: 86.7 us -> none
    all_to_all x3 -> x0, waiting for transfers between devices: 44.5 us -> none  [the longest x1 44.5 us: body(): lax.all_to_all(spread(own_in), 'expert', split_axis=0, concat_axis=0, til...]
    all_gather x1 -> x0, waiting for transfers between devices: 35.9 us -> none  [body(): lax.all_gather(stacked, 'dp', axis=0, tiled=True)]
    all_to_all x3 -> x0, starting transfers between devices: 35.5 us -> none  [the longest x1 15.3 us: body(): lax.all_to_all(spread(own_in), 'expert', split_axis=0, concat_axis=0, til...]
    all_gather x1 -> x0, blocking collectives: 27 us -> none  [body(): lax.all_gather(down_weight, 'dp', axis=1, tiled=True)]
    scatter x3 -> x0, local copies, waits for them, and re-layouts: 12.9 us -> none  [the longest x1 4.3 us: body(): jnp.zeros((per_device,), jnp.int32).at[local].set(token_of, mode='drop')]
    dot_general x5 -> x0, matrix products: 6.63 us -> none  [the longest x1 2.13 us: body(): jnp.dot(columns, lax.all_gather(stacked, 'dp', axis=0, tiled=True), prefe...]
  transfers between devices with their start and end apart: 5 -> 0, of which waited for: 3 -> 0; matrix products, arithmetic and copies ran while one was open for 5% -> 0% of each run, Pallas kernels for 0% -> 0%
where the time goes in v1:
time: 127 us; the launch traced here: 126 us
  Pallas kernels  116 us (91%)
  local copies, waits for them, and re-layouts  9.09 us (7%)
    pallas_call x1, Pallas kernels, body(): pl.pallas_call(kernel, out_shape=(jax.ShapeDtypeStruct((n_tok, width), bf...  116 us
    unnamed x20, local copies, waits for them, and re-layouts  9.09 us

profile of v1, /device:TPU:24, one launch (start us, length us, event | category | flops | bytes accessed | tf_op | source)
XLA Modules:
  0.0 125.5 jit_solution(14494610688904213175)
XLA Ops:
  0.6 0.0 copy-start.5
  0.6 0.7 copy-done.5
  1.3 0.0 copy-start
  1.3 1.0 copy-done
  2.4 0.0 copy-start.1
  2.4 1.0 copy-done.1
  3.4 0.0 copy-start.2
  3.4 0.8 copy-done.2
  4.2 0.0 copy-start.3
  4.2 0.8 copy-done.3
  4.9 0.0 copy-start.4
  4.9 0.8 copy-done.4
  5.7 0.0 copy-start.6
  5.7 0.7 copy-done.6
  6.4 0.0 copy-start.7
  6.4 0.7 copy-done.7
  7.1 115.8 %shard_map.111 = (bf16[128,2048]{1,0:T(8,128)(2,1)S(1)}, f32[64,192]{1,0:T(8,128)S(1)}, f32[64,192]{1,0:T(8,128)S(1)}, f32[64,192]{1,0:T(8,128)S(1)}) custom-call(bf16[128,2048]{1,0:T(8,128)(2,1)S(1)} %copy-done, bf16[128,2048]{1,0:T(8,128)(2,1)S(1)} %copy-done.1, s32[8,128]{1,0:T(8,128)S(1)} %bitcast.7, s32[8,128]{1,0:T(8,128)S(1)} %bitcast.8, ...), custom_call_target="tpu_custom_call" | custom-call | flops 1610612736 | bytes 2097152 | tf_op jit(solution)/shard_map/pallas_call | solution.py:610
  122.9 0.8 copy.16
  123.7 0.6 copy.17
  124.3 0.6 copy.18
  124.9 0.6 copy.19
Async XLA Ops:
  0.6 0.7 copy-start.5
  1.3 1.0 copy-start
  2.4 1.0 copy-start.1
  3.4 0.8 copy-start.2
  4.2 0.8 copy-start.3
  4.9 0.8 copy-start.4
  5.7 0.7 copy-start.6
  6.4 0.7 copy-start.7

commit v2 on v1

v2 whole, which is shorter than its diff:
```python
import functools

import jax
import jax.numpy as jnp
from jax import lax
from jax.experimental import pallas as pl
from jax.experimental.pallas import tpu as pltpu
from jax.sharding import PartitionSpec as P

MESH = pl.DeviceIdType.MESH
RING = 16
SPLIT = 4
CHIPS = SPLIT * SPLIT
CAP = 16
STEP = 256
LAST = (((1,), (1,)), ((), ()))
FIRST = (((0,), (0,)), ((), ()))


def copy_to(src, dst, send_sem, recv_sem, device):
    return pltpu.make_async_remote_copy(
        src_ref=src,
        dst_ref=dst,
        send_sem=send_sem,
        recv_sem=recv_sem,
        device_id=device,
        device_id_type=MESH,
    )


def kernel(
    tokens_hbm,
    cotangent_hbm,
    ids_hbm,
    mask_hbm,
    gates_hbm,
    gate_hbm,
    up_hbm,
    down_hbm,
    grad_tokens,
    grad_gate,
    grad_up,
    grad_down,
    tokens,
    cotangent,
    ids,
    mask,
    gates,
    gate_w,
    up_w,
    down_w,
    place,
    rows_in,
    rows_grad,
    out_in,
    out_grad,
    shards,
    weights,
    pre,
    act,
    pair,
    active,
    parts,
    returned,
    sums,
    finals,
    grads,
    sibling_grads,
    grads_in,
    group_sums,
    group_in,
    load_sem,
    entry_send,
    entry_recv,
    side_send,
    side_recv,
    shard_send,
    shard_recv,
    spread_send,
    spread_recv,
    twin_send,
    twin_recv,
    part_send,
    part_recv,
    final_send,
    final_recv,
    sibling_send,
    sibling_recv,
    grad_send,
    grad_recv,
    group_send,
    group_recv,
):
    width = tokens.shape[1]
    depth, hidden = gate_w.shape
    lanes = weights.shape[2]
    n_tok = tokens.shape[0]
    n_rows = RING * CAP
    blocks = STEP // depth
    chunks = width // STEP

    dp = lax.axis_index("dp")
    z = lax.axis_index("expert")
    group = z // SPLIT
    member = lax.rem(z, SPLIT)
    core = lax.rem(dp, 2)
    chip = dp // 2
    x = chip // SPLIT
    y = lax.rem(chip, SPLIT)
    sibling = (dp + 1 - 2 * core, z)

    def plane(offset):
        return (dp, lax.rem(z + offset + RING, RING))

    def at(to_x, to_y):
        return ((lax.rem(to_x + SPLIT, SPLIT) * SPLIT + lax.rem(to_y + SPLIT, SPLIT)) * 2 + core, z)

    up_down = 1 - 2 * core
    to_sides = (at(x + 1, y), at(x - 1, y), at(x, y + up_down))
    from_sides = (at(x - 1, y), at(x + 1, y), at(x, y - up_down))

    loads = [
        pltpu.make_async_copy(source, target, load_sem.at[i])
        for i, (source, target) in enumerate(
            (
                (ids_hbm, ids),
                (mask_hbm, mask),
                (gates_hbm, gates),
                (tokens_hbm, tokens),
                (cotangent_hbm, cotangent),
                (gate_hbm, gate_w),
                (up_hbm, up_w),
                (down_hbm, down_w),
            )
        )
    ]
    for load in loads:
        load.start()

    barrier = pltpu.get_barrier_semaphore()

    def greet_ring(i, carry):
        pl.semaphore_signal(barrier, inc=1, device_id=plane(i), device_id_type=MESH)
        return carry

    def greet_plane(i, carry):
        pl.semaphore_signal(
            barrier, inc=1, device_id=(lax.rem(dp + 2 * i, 2 * CHIPS), z), device_id_type=MESH
        )
        return carry

    lax.fori_loop(1, RING, greet_ring, 0)
    lax.fori_loop(1, CHIPS, greet_plane, 0)
    pl.semaphore_signal(barrier, inc=1, device_id=sibling, device_id_type=MESH)

    for load in loads[:3]:
        load.wait()
    live = mask[...] == 1
    hits, gate_rows = [], []
    for j in range(SPLIT):
        hit = jnp.where((ids[...] == j) & live, 1.0, 0.0)
        hits.append(jnp.sum(hit, axis=0, keepdims=True))
        gate_rows.append(jnp.sum(hit * gates[...], axis=0, keepdims=True))
    hit_rows = jnp.concatenate(hits + [jnp.zeros((CAP - SPLIT, n_tok), jnp.float32)], axis=0)
    earlier = (
        lax.broadcasted_iota(jnp.int32, (n_tok, n_tok), 0)
        < lax.broadcasted_iota(jnp.int32, (n_tok, n_tok), 1)
    )
    rank = jnp.dot(
        hit_rows.astype(jnp.bfloat16),
        jnp.where(earlier, 1.0, 0.0).astype(jnp.bfloat16),
        preferred_element_type=jnp.float32,
    )
    slot = lax.broadcasted_iota(jnp.int32, (CAP, n_tok), 0).astype(jnp.float32)
    slot_gates = []
    for j in range(SPLIT):
        held = jnp.where(
            (jnp.broadcast_to(rank[j : j + 1], (CAP, n_tok)) == slot)
            & (jnp.broadcast_to(hits[j], (CAP, n_tok)) > 0.5),
            1.0,
            0.0,
        )
        place[j] = held.astype(jnp.bfloat16)
        slot_gates.append(jnp.sum(held * gate_rows[j], axis=1, keepdims=True))
    slot_gate = jnp.concatenate(slot_gates, axis=0)
    chosen = place[...].reshape(SPLIT * CAP, n_tok)

    for load in loads[3:]:
        load.wait()

    def fill(c, carry):
        cols = pl.ds(pl.multiple_of(c * STEP, STEP), STEP)
        picked = jnp.dot(chosen, tokens[:, cols], preferred_element_type=jnp.float32)
        out_in[:, :, cols] = picked.astype(jnp.bfloat16).reshape(SPLIT, CAP, STEP)
        picked = jnp.dot(chosen, cotangent[:, cols], preferred_element_type=jnp.float32)
        out_grad[:, :, cols] = (
            (slot_gate * picked).astype(jnp.bfloat16).reshape(SPLIT, CAP, STEP)
        )
        return carry

    lax.fori_loop(0, chunks, fill, 0)
    rows_in[0, 0] = out_in[group]
    rows_grad[0, 0] = out_grad[group]

    packed = jnp.concatenate(
        [
            gate_w[...].astype(jnp.float32),
            up_w[...].astype(jnp.float32),
            down_w[...].astype(jnp.float32),
            jnp.zeros((depth, lanes - 3 * hidden), jnp.float32),
        ],
        axis=1,
    )
    shards[member] = packed.astype(jnp.bfloat16)

    pl.semaphore_wait(barrier, RING - 1 + CHIPS)

    both = ((out_in, rows_in), (out_grad, rows_grad))
    upper = member // 2
    edge = 1 - lax.rem((member + 1) // 2, 2)
    low = (1 - upper) * edge
    high = upper * edge
    entries = []
    for index, offset, place_there, expert in (
        (
            1,
            upper * (8 - member) - (1 - upper) * (member + 5),
            upper * member + (1 - upper) * (3 - member),
            lax.rem(group + 2, SPLIT),
        ),
        (0, 5 - member - low, member + low, lax.rem(group + 1, SPLIT)),
        (2, high - member - 2, 3 - member + high, lax.rem(group + 3, SPLIT)),
    ):
        for h, (source, rows) in enumerate(both):
            entries.append(
                copy_to(
                    source.at[expert],
                    rows.at[0, place_there],
                    entry_send.at[index, h],
                    entry_recv.at[place_there, h],
                    plane(offset),
                )
            )
    for copy in entries:
        copy.start()

    def shard_copy(i):
        return copy_to(
            shards.at[member],
            shards.at[member],
            shard_send.at[i],
            shard_recv.at[member],
            (dp, group * SPLIT + lax.rem(member + i, SPLIT)),
        )

    def spread_copy(part, to_y):
        to_x = lax.rem(part + 2 * to_y, SPLIT)
        return (
            (to_x * SPLIT + to_y) != chip,
            copy_to(
                shards.at[part],
                weights.at[dp],
                spread_send.at[part, to_y],
                spread_recv.at[chip],
                at(to_x, to_y),
            ),
        )

    def spread(i, carry):
        part = lax.rem(member + i, SPLIT)

        @pl.when(i > 0)
        def _():
            copy_to(
                shards.at[part], shards.at[part], shard_send.at[0], shard_recv.at[part], sibling
            ).wait_recv()

        for step in range(SPLIT):
            to_y = lax.rem(y + step, SPLIT)
            elsewhere, copy = spread_copy(part, to_y)
            pl.when(elsewhere)(copy.start)
        return carry

    for i in range(1, SPLIT):
        shard_copy(i).start()

    def side_copy(side, place_here, h):
        rows = both[h][1]
        return copy_to(
            rows.at[0, place_here],
            rows.at[1 + side, place_here],
            side_send.at[side, place_here, h],
            side_recv.at[side, place_here, h],
            to_sides[side],
        )

    def send_sides(place_here):
        for h in range(2):
            for side in range(3):
                side_copy(side, place_here, h).start()

    send_sides(0)
    lax.fori_loop(0, SPLIT, spread, 0)

    my_part = lax.rem(x + 2 * y, SPLIT)
    weights[dp] = shards[my_part]

    def twin_copy(i):
        index = lax.rem(chip + i, CHIPS) * 2 + core
        return copy_to(
            weights.at[index], weights.at[index], twin_send.at[i], twin_recv.at[i], sibling
        )

    twin_copy(0).start()

    def twin(i, carry):
        source = lax.rem(chip + i, CHIPS)
        copy_to(
            weights.at[source * 2 + core],
            weights.at[source * 2 + core],
            twin_send.at[i],
            spread_recv.at[source],
            sibling,
        ).wait_recv()
        twin_copy(i).start()
        return carry

    def pass_sides(place_here, carry):
        for h, (_, rows) in enumerate(both):
            copy_to(
                rows.at[0, place_here],
                rows.at[0, place_here],
                entry_send.at[0, h],
                entry_recv.at[place_here, h],
                sibling,
            ).wait_recv()
            for side in range(3):
                side_copy(side, place_here, h).start()
        return carry

    lax.fori_loop(1, SPLIT, pass_sides, 0)
    lax.fori_loop(1, CHIPS, twin, 0)

    def sides_arrived(place_here, carry):
        for side in range(3):
            for h, (_, rows) in enumerate(both):
                copy_to(
                    rows.at[1 + side, place_here],
                    rows.at[1 + side, place_here],
                    side_send.at[side, place_here, h],
                    side_recv.at[side, place_here, h],
                    sibling,
                ).wait_recv()
        return carry

    lax.fori_loop(0, SPLIT, sides_arrived, 0)

    def twins_arrived(i, carry):
        index = lax.rem(chip + i, CHIPS) * 2 + 1 - core
        copy_to(
            weights.at[index], weights.at[index], twin_send.at[i], twin_recv.at[i], sibling
        ).wait_recv()
        return carry

    lax.fori_loop(0, CHIPS, twins_arrived, 0)

    pre[...] = jnp.zeros_like(pre)
    act[...] = jnp.zeros_like(act)

    def project(c, carry):
        cols = pl.ds(pl.multiple_of(c * STEP, STEP), STEP)
        block = weights[pl.ds(c * blocks, blocks)].reshape(STEP, lanes)
        left = rows_in[:, :, :, cols].reshape(n_rows, STEP)
        pre[...] += jnp.dot(left, block[:, : 2 * hidden], preferred_element_type=jnp.float32)
        left = rows_grad[:, :, :, cols].reshape(n_rows, STEP)
        act[...] += jnp.dot(left, block[:, 2 * hidden :], preferred_element_type=jnp.float32)
        return carry

    lax.fori_loop(0, chunks, project, 0)

    pre_gate = pre[:, :hidden]
    pre_up = pre[:, hidden:]
    grad_act = act[:, :hidden]
    sigmoid_value = jax.nn.sigmoid(pre_gate)
    silu_value = pre_gate * sigmoid_value
    slope = sigmoid_value * (1.0 + pre_gate * (1.0 - sigmoid_value))
    pair[...] = jnp.concatenate(
        [grad_act * pre_up * slope, grad_act * silu_value], axis=1
    ).astype(jnp.bfloat16)
    active[...] = jnp.concatenate(
        [silu_value * pre_up, jnp.zeros((n_rows, act.shape[1] - hidden), jnp.float32)], axis=1
    ).astype(jnp.bfloat16)

    def back_project(c, carry):
        cols = pl.ds(pl.multiple_of(c * STEP, STEP), STEP)
        block = weights[pl.ds(c * blocks, blocks)].reshape(STEP, lanes)
        part = lax.dot_general(
            pair[...], block[:, : 2 * hidden], LAST, preferred_element_type=jnp.float32
        )
        parts[:, :, :, cols] = part.astype(jnp.bfloat16).reshape(SPLIT, SPLIT, CAP, STEP)
        return carry

    lax.fori_loop(0, chunks, back_project, 0)

    def part_copy(side, place_here):
        return copy_to(
            parts.at[1 + side, place_here],
            returned.at[side, place_here],
            part_send.at[side, place_here],
            part_recv.at[side, place_here],
            from_sides[side],
        )

    def send_parts(i, carry):
        for side in range(3):
            part_copy(side, lax.rem(i, SPLIT)).start()
        return carry

    lax.fori_loop(1, SPLIT + 1, send_parts, 0)

    def sibling_copy(i):
        some = pl.ds(i * SPLIT, SPLIT)
        return copy_to(
            grads.at[1 - core, some],
            sibling_grads.at[some],
            sibling_send.at[i],
            sibling_recv.at[i],
            sibling,
        )

    def weight_grads(i, carry):
        for half in range(2):
            c = 2 * i + half
            cols = pl.ds(pl.multiple_of(c * STEP, STEP), STEP)
            left = rows_in[:, :, :, cols].reshape(n_rows, STEP)
            one = lax.dot_general(left, pair[...], FIRST, preferred_element_type=jnp.float32)
            left = rows_grad[:, :, :, cols].reshape(n_rows, STEP)
            two = lax.dot_general(left, active[...], FIRST, preferred_element_type=jnp.float32)
            both_terms = jnp.concatenate([one, two], axis=1).astype(jnp.bfloat16)
            both_terms = both_terms.reshape(blocks, depth, lanes)
            for b in range(blocks):
                grads[b % 2, c * (blocks // 2) + b // 2] = both_terms[b]
        sibling_copy(i).start()
        return carry

    lax.fori_loop(0, SPLIT, weight_grads, 0)

    def sum_parts(place_here):
        for side in range(3):
            copy_to(
                returned.at[side, place_here],
                returned.at[side, place_here],
                part_send.at[side, place_here],
                part_recv.at[side, place_here],
                sibling,
            ).wait_recv()
        total = parts[0, place_here].astype(jnp.float32)
        for side in range(3):
            total += returned[side, place_here].astype(jnp.float32)
        sums[place_here] = total.astype(jnp.bfloat16)

    def final_copy(place_here):
        late = place_here // 2
        distance = edge * ((1 - late) * 4 + late * (8 - place_here)) + (1 - edge) * (5 - place_here)
        to = edge * late + (1 - edge * late) * 2 * upper
        return copy_to(
            sums.at[place_here],
            finals.at[to],
            final_send.at[place_here],
            final_recv.at[to],
            plane((2 * upper - 1) * distance),
        )

    def send_finals(place_here, carry):
        sum_parts(place_here)
        final_copy(place_here).start()
        return carry

    lax.fori_loop(1, SPLIT, send_finals, 0)

    def grad_copy(i):
        to = lax.rem(chip + i, CHIPS)
        return copy_to(
            grads.at[core, to],
            grads_in.at[chip],
            grad_send.at[i],
            grad_recv.at[chip],
            (2 * to + core, z),
        )

    def sibling_arrived(i, carry):
        some = pl.ds(i * SPLIT, SPLIT)
        copy_to(
            sibling_grads.at[some],
            sibling_grads.at[some],
            sibling_send.at[i],
            sibling_recv.at[i],
            sibling,
        ).wait_recv()
        return carry

    lax.fori_loop(0, SPLIT, sibling_arrived, 0)

    def chip_sum(to):
        return (
            grads[core, to].astype(jnp.float32) + sibling_grads[to].astype(jnp.float32)
        ).astype(jnp.bfloat16)

    grads_in[chip] = chip_sum(chip)

    def send_grads(i, carry):
        to = lax.rem(chip + i, CHIPS)
        grads[core, to] = chip_sum(to)
        grad_copy(i).start()
        return carry

    lax.fori_loop(1, CHIPS, send_grads, 0)

    sum_parts(0)

    def finals_arrived(i, carry):
        copy_to(
            finals.at[i], finals.at[i], final_send.at[1], final_recv.at[i], sibling
        ).wait_recv()
        return carry

    lax.fori_loop(0, 3, finals_arrived, 0)
    where_from = jnp.concatenate(
        [
            place[lax.rem(group + 1, SPLIT)],
            place[lax.rem(group + 2, SPLIT)],
            place[lax.rem(group + 3, SPLIT)],
            place[group],
        ],
        axis=0,
    )

    def give_back(c, carry):
        cols = pl.ds(pl.multiple_of(c * STEP, STEP), STEP)
        values = jnp.concatenate(
            [finals[:, :, cols].reshape(3 * CAP, STEP), sums[0, :, cols]], axis=0
        )
        grad_tokens[:, cols] = lax.dot_general(
            where_from, values, FIRST, preferred_element_type=jnp.float32
        ).astype(jnp.bfloat16)
        return carry

    lax.fori_loop(0, chunks, give_back, 0)

    def plane_sum(part):
        total = jnp.zeros((depth, lanes), jnp.float32)
        for from_y in range(SPLIT):
            source = lax.rem(part + 2 * from_y, SPLIT) * SPLIT + from_y

            @pl.when(source != chip)
            def _():
                copy_to(
                    grads_in.at[source],
                    grads_in.at[source],
                    grad_send.at[0],
                    grad_recv.at[source],
                    sibling,
                ).wait_recv()

            total += grads_in[source].astype(jnp.float32)
        return total

    def group_copy(i):
        part = lax.rem(member + i, SPLIT)
        return copy_to(
            group_sums.at[i],
            group_in.at[SPLIT - i],
            group_send.at[i],
            group_recv.at[SPLIT - i],
            (dp, group * SPLIT + part),
        )

    def send_group(i, carry):
        group_sums[i] = plane_sum(lax.rem(member + i, SPLIT)).astype(jnp.bfloat16)
        group_copy(i).start()
        return carry

    lax.fori_loop(1, SPLIT, send_group, 0)
    total = plane_sum(member)
    for i in range(1, SPLIT):
        copy_to(
            group_in.at[i], group_in.at[i], group_send.at[i], group_recv.at[i], sibling
        ).wait_recv()
        total += group_in[i].astype(jnp.float32)
    grad_gate[...] = total[:, :hidden]
    grad_up[...] = total[:, hidden : 2 * hidden]
    grad_down[...] = total[:, 2 * hidden : 3 * hidden]

    for copy in entries:
        copy.wait_send()

    def drain_places(place_here, carry):
        for side in range(3):
            part_copy(side, place_here).wait_send()
            for h in range(2):
                side_copy(side, place_here, h).wait_send()
        return carry

    lax.fori_loop(0, SPLIT, drain_places, 0)

    def drain_spread(part, carry):
        for to_y in range(SPLIT):
            elsewhere, copy = spread_copy(part, to_y)
            pl.when(elsewhere)(copy.wait_send)
        sibling_copy(part).wait_send()
        return carry

    lax.fori_loop(0, SPLIT, drain_spread, 0)

    def drain_some(i, carry):
        shard_copy(i).wait_send()
        final_copy(i).wait_send()
        group_copy(i).wait_send()
        return carry

    lax.fori_loop(1, SPLIT, drain_some, 0)
    twin_copy(0).wait_send()

    def drain_chips(i, carry):
        twin_copy(i).wait_send()
        grad_copy(i).wait_send()
        return carry

    lax.fori_loop(1, CHIPS, drain_chips, 0)


def body(tokens, cotangent, ids, mask, gates, gate_w, up_w, down_w):
    n_tok, width = tokens.shape
    top = ids.shape[1]
    depth, hidden = gate_w.shape
    lanes = -(-3 * hidden // 128) * 128
    n_rows = RING * CAP
    bf16, f32, i32 = jnp.bfloat16, jnp.float32, jnp.int32
    vmem = pl.BlockSpec(memory_space=pltpu.VMEM)
    dma = pltpu.SemaphoreType.DMA
    grad_tokens, grad_gate, grad_up, grad_down = pl.pallas_call(
        kernel,
        out_shape=(
            jax.ShapeDtypeStruct((n_tok, width), bf16),
            jax.ShapeDtypeStruct((depth, hidden), f32),
            jax.ShapeDtypeStruct((depth, hidden), f32),
            jax.ShapeDtypeStruct((depth, hidden), f32),
        ),
        in_specs=[pl.BlockSpec(memory_space=pl.ANY)] * 8,
        out_specs=[vmem] * 4,
        scratch_shapes=[
            pltpu.VMEM((n_tok, width), bf16),
            pltpu.VMEM((n_tok, width), bf16),
            pltpu.VMEM((top, n_tok), i32),
            pltpu.VMEM((top, n_tok), i32),
            pltpu.VMEM((top, n_tok), f32),
            pltpu.VMEM((depth, hidden), bf16),
            pltpu.VMEM((depth, hidden), bf16),
            pltpu.VMEM((depth, hidden), bf16),
            pltpu.VMEM((SPLIT, CAP, n_tok), bf16),
            pltpu.VMEM((SPLIT, SPLIT, CAP, width), bf16),
            pltpu.VMEM((SPLIT, SPLIT, CAP, width), bf16),
            pltpu.VMEM((SPLIT, CAP, width), bf16),
            pltpu.VMEM((SPLIT, CAP, width), bf16),
            pltpu.VMEM((SPLIT, depth, lanes), bf16),
            pltpu.VMEM((2 * CHIPS, depth, lanes), bf16),
            pltpu.VMEM((n_rows, 2 * hidden), f32),
            pltpu.VMEM((n_rows, lanes - 2 * hidden), f32),
            pltpu.VMEM((n_rows, 2 * hidden), bf16),
            pltpu.VMEM((n_rows, lanes - 2 * hidden), bf16),
            pltpu.VMEM((SPLIT, SPLIT, CAP, width), bf16),
            pltpu.VMEM((3, SPLIT, CAP, width), bf16),
            pltpu.VMEM((SPLIT, CAP, width), bf16),
            pltpu.VMEM((3, CAP, width), bf16),
            pltpu.VMEM((2, CHIPS, depth, lanes), bf16),
            pltpu.VMEM((CHIPS, depth, lanes), bf16),
            pltpu.VMEM((CHIPS, depth, lanes), bf16),
            pltpu.VMEM((SPLIT, depth, lanes), bf16),
            pltpu.VMEM((SPLIT, depth, lanes), bf16),
            dma((8,)),
            dma((3, 2)),
            dma((SPLIT, 2)),
            dma((3, SPLIT, 2)),
            dma((3, SPLIT, 2)),
            dma((SPLIT,)),
            dma((SPLIT,)),
            dma((SPLIT, SPLIT)),
            dma((CHIPS,)),
            dma((CHIPS,)),
            dma((CHIPS,)),
            dma((3, SPLIT)),
            dma((3, SPLIT)),
            dma((SPLIT,)),
            dma((3,)),
            dma((SPLIT,)),
            dma((SPLIT,)),
            dma((CHIPS,)),
            dma((CHIPS,)),
            dma((SPLIT,)),
            dma((SPLIT,)),
        ],
        compiler_params=pltpu.CompilerParams(
            collective_id=0, has_side_effects=True, vmem_limit_bytes=48 * 1024 * 1024
        ),
        cost_estimate=pl.CostEstimate(
            flops=16 * n_rows * width * hidden, bytes_accessed=1 << 21, transcendentals=1 << 16
        ),
    )(tokens, cotangent, ids.T, mask.T, gates.T, gate_w, up_w, down_w.T)
    return grad_tokens, grad_gate, grad_up, grad_down.T


def solution(mesh):
    rows = P(("dp", "expert"), None)
    return jax.shard_map(
        body,
        mesh=mesh,
        in_specs=(rows, rows, rows, rows, rows) + (P("dp", "expert"),) * 2 + (P("expert", "dp"),),
        out_specs=(rows, P("dp", "expert"), P("dp", "expert"), P("expert", "dp")),
        check_vma=False,
    )
```

time: 127 us -> 111 us (0.87)
  Pallas kernels: 116 us -> 99.4 us
    pallas_call x1, Pallas kernels: 116 us -> 99.4 us  [body(): pl.pallas_call(kernel, out_shape=(jax.ShapeDtypeStruct((n_tok, width), bf...]
where the time goes in v2:
time: 111 us; the launch traced here: 109 us
  Pallas kernels  99.4 us (90%)
  local copies, waits for them, and re-layouts  9.09 us (8%)
    pallas_call x1, Pallas kernels, body(): pl.pallas_call(kernel, out_shape=(jax.ShapeDtypeStruct((n_tok, width), bf...  99.4 us
    unnamed x20, local copies, waits for them, and re-layouts  9.09 us

profile of v2, /device:TPU:24, one launch (start us, length us, event | category | flops | bytes accessed | tf_op | source)
XLA Modules:
  0.0 109.1 jit_solution(4583296932489952844)
XLA Ops:
  0.6 0.0 copy-start.5
  0.6 0.7 copy-done.5
  1.3 0.0 copy-start
  1.3 1.0 copy-done
  2.4 0.0 copy-start.1
  2.4 1.0 copy-done.1
  3.4 0.0 copy-start.2
  3.4 0.8 copy-done.2
  4.2 0.0 copy-start.3
  4.2 0.8 copy-done.3
  4.9 0.0 copy-start.4
  4.9 0.8 copy-done.4
  5.7 0.0 copy-start.6
  5.7 0.7 copy-done.6
  6.4 0.0 copy-start.7
  6.4 0.7 copy-done.7
  7.1 99.4 %shard_map.111 = (bf16[128,2048]{1,0:T(8,128)(2,1)S(1)}, f32[64,192]{1,0:T(8,128)S(1)}, f32[64,192]{1,0:T(8,128)S(1)}, f32[64,192]{1,0:T(8,128)S(1)}) custom-call(bf16[128,2048]{1,0:T(8,128)(2,1)S(1)} %copy-done, bf16[128,2048]{1,0:T(8,128)(2,1)S(1)} %copy-done.1, s32[8,128]{1,0:T(8,128)S(1)} %bitcast.7, s32[8,128]{1,0:T(8,128)S(1)} %bitcast.8, ...), custom_call_target="tpu_custom_call" | custom-call | flops 1610612736 | bytes 2097152 | tf_op jit(solution)/shard_map/pallas_call | solution.py:641
  106.5 0.8 copy.16
  107.2 0.6 copy.17
  107.9 0.6 copy.18
  108.5 0.6 copy.19
Async XLA Ops:
  0.6 0.7 copy-start.5
  1.3 1.0 copy-start
  2.4 1.0 copy-start.1
  3.4 0.8 copy-start.2
  4.2 0.8 copy-start.3
  4.9 0.8 copy-start.4
  5.7 0.7 copy-start.6
  6.4 0.7 copy-start.7

commit v3 on v2

--- a/solution.py
+++ b/solution.py
@@ -12,7 +12,8 @@
 SPLIT = 4
 CHIPS = SPLIT * SPLIT
 CAP = 16
-STEP = 256
+STEP = 512
+PIECES = 2
 LAST = (((1,), (1,)), ((), ()))
 FIRST = (((0,), (0,)), ((), ()))
 
@@ -26,6 +27,11 @@
         device_id=device,
         device_id_type=MESH,
     )
+
+
+def beside(left, right):
+    both = [left.astype(jnp.float32), right.astype(jnp.float32)]
+    return jnp.concatenate(both, axis=-1).astype(jnp.bfloat16)
 
 
 def kernel(
@@ -93,7 +99,8 @@
 ):
     width = tokens.shape[1]
     depth, hidden = gate_w.shape
-    lanes = weights.shape[2]
+    tall = weights.shape[1]
+    piece = tall // PIECES
     n_tok = tokens.shape[0]
     n_rows = RING * CAP
     blocks = STEP // depth
@@ -202,16 +209,8 @@
     rows_in[0, 0] = out_in[group]
     rows_grad[0, 0] = out_grad[group]
 
-    packed = jnp.concatenate(
-        [
-            gate_w[...].astype(jnp.float32),
-            up_w[...].astype(jnp.float32),
-            down_w[...].astype(jnp.float32),
-            jnp.zeros((depth, lanes - 3 * hidden), jnp.float32),
-        ],
-        axis=1,
-    )
-    shards[member] = packed.astype(jnp.bfloat16)
+    shards[member, :depth] = beside(gate_w[...], up_w[...])
+    shards[member, depth:] = beside(down_w[: depth // 2], down_w[depth // 2 :])
 
     pl.semaphore_wait(barrier, RING - 1 + CHIPS)
 
@@ -241,48 +240,61 @@
                     plane(offset),
                 )
             )
-    for copy in entries:
-        copy.start()
-
-    def shard_copy(i):
+
+    def rows_of(h):
+        return pl.ds(h * piece, piece)
+
+    def shard_copy(i, h):
         return copy_to(
-            shards.at[member],
-            shards.at[member],
-            shard_send.at[i],
-            shard_recv.at[member],
+            shards.at[member, rows_of(h)],
+            shards.at[member, rows_of(h)],
+            shard_send.at[i, h],
+            shard_recv.at[member, h],
             (dp, group * SPLIT + lax.rem(member + i, SPLIT)),
         )
 
-    def spread_copy(part, to_y):
+    def spread_copy(part, to_y, h):
         to_x = lax.rem(part + 2 * to_y, SPLIT)
         return (
             (to_x * SPLIT + to_y) != chip,
             copy_to(
-                shards.at[part],
-                weights.at[dp],
-                spread_send.at[part, to_y],
-                spread_recv.at[chip],
+                shards.at[part, rows_of(h)],
+                weights.at[dp, rows_of(h)],
+                spread_send.at[part, to_y, h],
+                spread_recv.at[chip, h],
                 at(to_x, to_y),
             ),
         )
 
-    def spread(i, carry):
+    def spread(h, i):
         part = lax.rem(member + i, SPLIT)
 
         @pl.when(i > 0)
         def _():
+            some = shards.at[part, rows_of(h)]
             copy_to(
-                shards.at[part], shards.at[part], shard_send.at[0], shard_recv.at[part], sibling
+                some, some, shard_send.at[0, h], shard_recv.at[part, h], sibling
             ).wait_recv()
 
         for step in range(SPLIT):
             to_y = lax.rem(y + step, SPLIT)
-            elsewhere, copy = spread_copy(part, to_y)
+            elsewhere, copy = spread_copy(part, to_y, h)
             pl.when(elsewhere)(copy.start)
-        return carry
-
-    for i in range(1, SPLIT):
-        shard_copy(i).start()
+
+    def spread_rest(n, carry):
+        spread(n // 3, 1 + lax.rem(n, 3))
+        return carry
+
+    def spread_own(h, carry):
+        spread(h, 0)
+        return carry
+
+    for h in range(PIECES):
+        for i in range(1, SPLIT):
+            shard_copy(i, h).start()
+    for copy in entries:
+        copy.start()
+
 
     def side_copy(side, place_here, h):
         rows = both[h][1]
@@ -300,30 +312,30 @@
                 side_copy(side, place_here, h).start()
 
     send_sides(0)
-    lax.fori_loop(0, SPLIT, spread, 0)
+    lax.fori_loop(0, PIECES, spread_own, 0)
+    lax.fori_loop(0, 3 * PIECES, spread_rest, 0)
 
     my_part = lax.rem(x + 2 * y, SPLIT)
     weights[dp] = shards[my_part]
 
-    def twin_copy(i):
-        index = lax.rem(chip + i, CHIPS) * 2 + core
-        return copy_to(
-            weights.at[index], weights.at[index], twin_send.at[i], twin_recv.at[i], sibling
-        )
-
-    twin_copy(0).start()
-
-    def twin(i, carry):
-        source = lax.rem(chip + i, CHIPS)
-        copy_to(
-            weights.at[source * 2 + core],
-            weights.at[source * 2 + core],
-            twin_send.at[i],
-            spread_recv.at[source],
-            sibling,
-        ).wait_recv()
-        twin_copy(i).start()
-        return carry
+    def twin_copy(i, h):
+        some = weights.at[lax.rem(chip + i, CHIPS) * 2 + core, rows_of(h)]
+        return copy_to(some, some, twin_send.at[i, h], twin_recv.at[i, h], sibling)
+
+    for h in range(PIECES):
+        twin_copy(0, h).start()
+
+    def twin(h):
+        def one(i, carry):
+            source = lax.rem(chip + i, CHIPS)
+            some = weights.at[source * 2 + core, rows_of(h)]
+            copy_to(
+                some, some, twin_send.at[i, h], spread_recv.at[source, h], sibling
+            ).wait_recv()
+            twin_copy(i, h).start()
+            return carry
+
+        lax.fori_loop(1, CHIPS, one, 0)
 
     def pass_sides(place_here, carry):
         for h, (_, rows) in enumerate(both):
@@ -338,8 +350,11 @@
                 side_copy(side, place_here, h).start()
         return carry
 
-    lax.fori_loop(1, SPLIT, pass_sides, 0)
-    lax.fori_loop(1, CHIPS, twin, 0)
+    pass_sides(1, 0)
+    twin(0)
+    pass_sides(2, 0)
+    pass_sides(3, 0)
+    twin(1)
 
     def sides_arrived(place_here, carry):
         for side in range(3):
@@ -356,10 +371,9 @@
     lax.fori_loop(0, SPLIT, sides_arrived, 0)
 
     def twins_arrived(i, carry):
-        index = lax.rem(chip + i, CHIPS) * 2 + 1 - core
-        copy_to(
-            weights.at[index], weights.at[index], twin_send.at[i], twin_recv.at[i], sibling
-        ).wait_recv()
+        for h in range(PIECES):
+            some = weights.at[lax.rem(chip + i, CHIPS) * 2 + 1 - core, rows_of(h)]
+            copy_to(some, some, twin_send.at[i, h], twin_recv.at[i, h], sibling).wait_recv()
         return carry
 
     lax.fori_loop(0, CHIPS, twins_arrived, 0)
@@ -369,34 +383,35 @@
 
     def project(c, carry):
         cols = pl.ds(pl.multiple_of(c * STEP, STEP), STEP)
-        block = weights[pl.ds(c * blocks, blocks)].reshape(STEP, lanes)
+        some = pl.ds(c * blocks, blocks)
+        block = weights[some, :depth].reshape(STEP, 2 * hidden)
         left = rows_in[:, :, :, cols].reshape(n_rows, STEP)
-        pre[...] += jnp.dot(left, block[:, : 2 * hidden], preferred_element_type=jnp.float32)
+        pre[...] += jnp.dot(left, block, preferred_element_type=jnp.float32)
+        below = weights[some, depth:]
+        block = jnp.concatenate([below[:, :, :hidden], below[:, :, hidden:]], axis=1)
         left = rows_grad[:, :, :, cols].reshape(n_rows, STEP)
-        act[...] += jnp.dot(left, block[:, 2 * hidden :], preferred_element_type=jnp.float32)
+        act[...] += jnp.dot(
+            left, block.reshape(STEP, hidden), preferred_element_type=jnp.float32
+        )
         return carry
 
     lax.fori_loop(0, chunks, project, 0)
 
     pre_gate = pre[:, :hidden]
     pre_up = pre[:, hidden:]
-    grad_act = act[:, :hidden]
+    grad_act = act[...]
     sigmoid_value = jax.nn.sigmoid(pre_gate)
     silu_value = pre_gate * sigmoid_value
     slope = sigmoid_value * (1.0 + pre_gate * (1.0 - sigmoid_value))
     pair[...] = jnp.concatenate(
         [grad_act * pre_up * slope, grad_act * silu_value], axis=1
     ).astype(jnp.bfloat16)
-    active[...] = jnp.concatenate(
-        [silu_value * pre_up, jnp.zeros((n_rows, act.shape[1] - hidden), jnp.float32)], axis=1
-    ).astype(jnp.bfloat16)
+    active[...] = (silu_value * pre_up).astype(jnp.bfloat16)
 
     def back_project(c, carry):
         cols = pl.ds(pl.multiple_of(c * STEP, STEP), STEP)
-        block = weights[pl.ds(c * blocks, blocks)].reshape(STEP, lanes)
-        part = lax.dot_general(
-            pair[...], block[:, : 2 * hidden], LAST, preferred_element_type=jnp.float32
-        )
+        block = weights[pl.ds(c * blocks, blocks), :depth].reshape(STEP, 2 * hidden)
+        part = lax.dot_general(pair[...], block, LAST, preferred_element_type=jnp.float32)
         parts[:, :, :, cols] = part.astype(jnp.bfloat16).reshape(SPLIT, SPLIT, CAP, STEP)
         return carry
 
@@ -429,17 +444,19 @@
         )
 
     def weight_grads(i, carry):
-        for half in range(2):
-            c = 2 * i + half
+        for half in range(1):
+            c = i + half
             cols = pl.ds(pl.multiple_of(c * STEP, STEP), STEP)
             left = rows_in[:, :, :, cols].reshape(n_rows, STEP)
             one = lax.dot_general(left, pair[...], FIRST, preferred_element_type=jnp.float32)
             left = rows_grad[:, :, :, cols].reshape(n_rows, STEP)
             two = lax.dot_general(left, active[...], FIRST, preferred_element_type=jnp.float32)
-            both_terms = jnp.concatenate([one, two], axis=1).astype(jnp.bfloat16)
-            both_terms = both_terms.reshape(blocks, depth, lanes)
+            one = one.astype(jnp.bfloat16).reshape(blocks, depth, 2 * hidden)
+            two = two.reshape(blocks, 2, depth // 2, hidden)
             for b in range(blocks):
-                grads[b % 2, c * (blocks // 2) + b // 2] = both_terms[b]
+                to = c * (blocks // 2) + b // 2
+                grads[b % 2, to, :depth] = one[b]
+                grads[b % 2, to, depth:] = beside(two[b, 0], two[b, 1])
         sibling_copy(i).start()
         return carry
 
@@ -478,13 +495,13 @@
 
     lax.fori_loop(1, SPLIT, send_finals, 0)
 
-    def grad_copy(i):
+    def grad_copy(i, h):
         to = lax.rem(chip + i, CHIPS)
         return copy_to(
-            grads.at[core, to],
-            grads_in.at[chip],
-            grad_send.at[i],
-            grad_recv.at[chip],
+            grads.at[core, to, rows_of(h)],
+            grads_in.at[chip, rows_of(h)],
+            grad_send.at[i, h],
+            grad_recv.at[chip, h],
             (2 * to + core, z),
         )
 
@@ -511,10 +528,17 @@
     def send_grads(i, carry):
         to = lax.rem(chip + i, CHIPS)
         grads[core, to] = chip_sum(to)
-        grad_copy(i).start()
+        grad_copy(i, 0).start()
         return carry
 
     lax.fori_loop(1, CHIPS, send_grads, 0)
+
+    def send_later(i, carry):
+        for h in range(1, PIECES):
+            grad_copy(i, h).start()
+        return carry
+
+    lax.fori_loop(1, CHIPS, send_later, 0)
 
     sum_parts(0)
 
@@ -547,49 +571,46 @@
 
     lax.fori_loop(0, chunks, give_back, 0)
 
-    def plane_sum(part):
-        total = jnp.zeros((depth, lanes), jnp.float32)
+    def plane_sum(part, h):
+        total = jnp.zeros((piece, 2 * hidden), jnp.float32)
         for from_y in range(SPLIT):
             source = lax.rem(part + 2 * from_y, SPLIT) * SPLIT + from_y
 
             @pl.when(source != chip)
             def _():
-                copy_to(
-                    grads_in.at[source],
-                    grads_in.at[source],
-                    grad_send.at[0],
-                    grad_recv.at[source],
-                    sibling,
-                ).wait_recv()
-
-            total += grads_in[source].astype(jnp.float32)
+                some = grads_in.at[source, rows_of(h)]
+                copy_to(some, some, grad_send.at[0, h], grad_recv.at[source, h], sibling).wait_recv()
+
+            total += grads_in[source, rows_of(h)].astype(jnp.float32)
         return total
 
-    def group_copy(i):
+    def group_copy(i, h):
         part = lax.rem(member + i, SPLIT)
         return copy_to(
-            group_sums.at[i],
-            group_in.at[SPLIT - i],
-            group_send.at[i],
-            group_recv.at[SPLIT - i],
+            group_sums.at[i, rows_of(h)],
+            group_in.at[SPLIT - i, rows_of(h)],
+            group_send.at[i, h],
+            group_recv.at[SPLIT - i, h],
             (dp, group * SPLIT + part),
         )
 
-    def send_group(i, carry):
-        group_sums[i] = plane_sum(lax.rem(member + i, SPLIT)).astype(jnp.bfloat16)
-        group_copy(i).start()
-        return carry
-
-    lax.fori_loop(1, SPLIT, send_group, 0)
-    total = plane_sum(member)
+    def send_group(n, carry):
+        h, i = n // 3, 1 + lax.rem(n, 3)
+        group_sums[i, rows_of(h)] = plane_sum(lax.rem(member + i, SPLIT), h).astype(jnp.bfloat16)
+        group_copy(i, h).start()
+        return carry
+
+    lax.fori_loop(0, 3 * PIECES, send_group, 0)
+    total = jnp.concatenate([plane_sum(member, h) for h in range(PIECES)], axis=0)
     for i in range(1, SPLIT):
-        copy_to(
-            group_in.at[i], group_in.at[i], group_send.at[i], group_recv.at[i], sibling
-        ).wait_recv()
+        for h in range(PIECES):
+            some = group_in.at[i, rows_of(h)]
+            copy_to(some, some, group_send.at[i, h], group_recv.at[i, h], sibling).wait_recv()
         total += group_in[i].astype(jnp.float32)
-    grad_gate[...] = total[:, :hidden]
-    grad_up[...] = total[:, hidden : 2 * hidden]
-    grad_down[...] = total[:, 2 * hidden : 3 * hidden]
+    grad_gate[...] = total[:depth, :hidden]
+    grad_up[...] = total[:depth, hidden:]
+    grad_down[: depth // 2] = total[depth:, :hidden]
+    grad_down[depth // 2 :] = total[depth:, hidden:]
 
     for copy in entries:
         copy.wait_send()
@@ -605,25 +626,29 @@
 
     def drain_spread(part, carry):
         for to_y in range(SPLIT):
-            elsewhere, copy = spread_copy(part, to_y)
-            pl.when(elsewhere)(copy.wait_send)
+            for h in range(PIECES):
+                elsewhere, copy = spread_copy(part, to_y, h)
+                pl.when(elsewhere)(copy.wait_send)
         sibling_copy(part).wait_send()
         return carry
 
     lax.fori_loop(0, SPLIT, drain_spread, 0)
 
     def drain_some(i, carry):
-        shard_copy(i).wait_send()
         final_copy(i).wait_send()
-        group_copy(i).wait_send()
+        for h in range(PIECES):
+            shard_copy(i, h).wait_send()
+            group_copy(i, h).wait_send()
         return carry
 
     lax.fori_loop(1, SPLIT, drain_some, 0)
-    twin_copy(0).wait_send()
+    for h in range(PIECES):
+        twin_copy(0, h).wait_send()
 
     def drain_chips(i, carry):
-        twin_copy(i).wait_send()
-        grad_copy(i).wait_send()
+        for h in range(PIECES):
+            twin_copy(i, h).wait_send()
+            grad_copy(i, h).wait_send()
         return carry
 
     lax.fori_loop(1, CHIPS, drain_chips, 0)
@@ -633,7 +658,7 @@
     n_tok, width = tokens.shape
     top = ids.shape[1]
     depth, hidden = gate_w.shape
-    lanes = -(-3 * hidden // 128) * 128
+    tall = depth * 3 // 2
     n_rows = RING * CAP
     bf16, f32, i32 = jnp.bfloat16, jnp.float32, jnp.int32
     vmem = pl.BlockSpec(memory_space=pltpu.VMEM)
@@ -646,7 +671,7 @@
             jax.ShapeDtypeStruct((depth, hidden), f32),
             jax.ShapeDtypeStruct((depth, hidden), f32),
         ),
-        in_specs=[pl.BlockSpec(memory_space=pl.ANY)] * 8,
+        in_specs=[pl.BlockSpec(memory_space=pltpu.HBM)] * 8,
         out_specs=[vmem] * 4,
         scratch_shapes=[
             pltpu.VMEM((n_tok, width), bf16),
@@ -662,45 +687,45 @@
             pltpu.VMEM((SPLIT, SPLIT, CAP, width), bf16),
             pltpu.VMEM((SPLIT, CAP, width), bf16),
             pltpu.VMEM((SPLIT, CAP, width), bf16),
-            pltpu.VMEM((SPLIT, depth, lanes), bf16),
-            pltpu.VMEM((2 * CHIPS, depth, lanes), bf16),
+            pltpu.VMEM((SPLIT, tall, 2 * hidden), bf16),
+            pltpu.VMEM((2 * CHIPS, tall, 2 * hidden), bf16),
             pltpu.VMEM((n_rows, 2 * hidden), f32),
-            pltpu.VMEM((n_rows, lanes - 2 * hidden), f32),
+            pltpu.VMEM((n_rows, hidden), f32),
             pltpu.VMEM((n_rows, 2 * hidden), bf16),
-            pltpu.VMEM((n_rows, lanes - 2 * hidden), bf16),
+            pltpu.VMEM((n_rows, hidden), bf16),
             pltpu.VMEM((SPLIT, SPLIT, CAP, width), bf16),
             pltpu.VMEM((3, SPLIT, CAP, width), bf16),
             pltpu.VMEM((SPLIT, CAP, width), bf16),
             pltpu.VMEM((3, CAP, width), bf16),
-            pltpu.VMEM((2, CHIPS, depth, lanes), bf16),
-            pltpu.VMEM((CHIPS, depth, lanes), bf16),
-            pltpu.VMEM((CHIPS, depth, lanes), bf16),
-            pltpu.VMEM((SPLIT, depth, lanes), bf16),
-            pltpu.VMEM((SPLIT, depth, lanes), bf16),
+            pltpu.VMEM((2, CHIPS, tall, 2 * hidden), bf16),
+            pltpu.VMEM((CHIPS, tall, 2 * hidden), bf16),
+            pltpu.VMEM((CHIPS, tall, 2 * hidden), bf16),
+            pltpu.VMEM((SPLIT, tall, 2 * hidden), bf16),
+            pltpu.VMEM((SPLIT, tall, 2 * hidden), bf16),
             dma((8,)),
             dma((3, 2)),
             dma((SPLIT, 2)),
             dma((3, SPLIT, 2)),
             dma((3, SPLIT, 2)),
-            dma((SPLIT,)),
-            dma((SPLIT,)),
-            dma((SPLIT, SPLIT)),
-            dma((CHIPS,)),
-            dma((CHIPS,)),
-            dma((CHIPS,)),
+            dma((SPLIT, PIECES)),
+            dma((SPLIT, PIECES)),
+            dma((SPLIT, SPLIT, PIECES)),
+            dma((CHIPS, PIECES)),
+            dma((CHIPS, PIECES)),
+            dma((CHIPS, PIECES)),
             dma((3, SPLIT)),
             dma((3, SPLIT)),
             dma((SPLIT,)),
             dma((3,)),
             dma((SPLIT,)),
             dma((SPLIT,)),
-            dma((CHIPS,)),
-            dma((CHIPS,)),
-            dma((SPLIT,)),
-            dma((SPLIT,)),
+            dma((CHIPS, PIECES)),
+            dma((CHIPS, PIECES)),
+            dma((SPLIT, PIECES)),
+            dma((SPLIT, PIECES)),
         ],
         compiler_params=pltpu.CompilerParams(
-            collective_id=0, has_side_effects=True, vmem_limit_bytes=48 * 1024 * 1024
+            collective_id=0, has_side_effects=True, vmem_limit_bytes=64 * 1024 * 1024 - 131072
         ),
         cost_estimate=pl.CostEstimate(
             flops=16 * n_rows * width * hidden, bytes_accessed=1 << 21, transcendentals=1 << 16

time: 111 us -> 84.6 us (0.76); the launches traced: 109 us -> 84.3 us
  Pallas kernels: 99.4 us -> 79.4 us
  local copies, waits for them, and re-layouts: 9.09 us -> 4.27 us
    pallas_call x1, Pallas kernels: 99.4 us -> 79.4 us  [body(): pl.pallas_call(kernel, out_shape=(jax.ShapeDtypeStruct((n_tok, width), bf...]
    unnamed x20 -> x10, local copies, waits for them, and re-layouts: 9.09 us -> 4.27 us
where the time goes in v3:
time: 84.6 us; the launch traced here: 84.3 us
  Pallas kernels  79.4 us (94%)
  local copies, waits for them, and re-layouts  4.27 us (5%)
    pallas_call x1, Pallas kernels, body(): pl.pallas_call(kernel, out_shape=(jax.ShapeDtypeStruct((n_tok, width), bf...  79.4 us
    unnamed x10, local copies, waits for them, and re-layouts  4.27 us

profile of v3, /device:TPU:24, one launch (start us, length us, event | category | flops | bytes accessed | tf_op | source)
XLA Modules:
  0.0 84.3 jit_solution(16311968424318426636)
XLA Ops:
  0.6 79.4 %shard_map.111 = (bf16[128,2048]{1,0:T(8,128)(2,1)}, f32[64,192]{1,0:T(8,128)}, f32[64,192]{1,0:T(8,128)}, f32[64,192]{1,0:T(8,128)}) custom-call(bf16[128,2048]{1,0:T(8,128)(2,1)} %tokens_hbm.1, bf16[128,2048]{1,0:T(8,128)(2,1)} %cotangent_hbm.1, s32[8,128]{1,0:T(8,128)} %bitcast.7, s32[8,128]{1,0:T(8,128)} %bitcast.8, f32[8,128]{1,0:T(8,128)} %bitcast.9, ...), custom_call_target="tpu_custom_call" | custom-call | flops 1610612736 | bytes 2097152 | tf_op jit(solution)/shard_map/pallas_call | solution.py:666
  80.0 0.0 copy-start.2
  80.0 1.9 %copy.16 = bf16[128,2048]{1,0:T(8,128)(2,1)} copy(bf16[128,2048]{1,0:T(8,128)(2,1)} %get-tuple-element.16) | data formatting | bytes 1048576
  81.9 0.0 copy-done.2
  81.9 0.0 copy-start.1
  81.9 0.6 copy.17
  82.6 0.2 copy-done.1
  82.8 0.0 copy-start
  82.8 0.6 copy.18
  83.4 0.2 copy-done
  83.7 0.6 copy.19
Async XLA Ops:
  80.0 1.9 %copy-start.2 = (f32[64,192]{1,0:T(8,128)S(1)}, f32[64,192]{1,0:T(8,128)}, u32[]{:S(2)}) copy-start(f32[64,192]{1,0:T(8,128)} %get-tuple-element.17) | copy-start | bytes 147460
  81.9 0.9 %copy-start.1 = (f32[64,192]{1,0:T(8,128)S(1)}, f32[64,192]{1,0:T(8,128)}, u32[]{:S(2)}) copy-start(f32[64,192]{1,0:T(8,128)} %get-tuple-element.18) | copy-start | bytes 147460
  82.8 0.9 %copy-start = (f32[64,192]{1,0:T(8,128)S(1)}, f32[64,192]{1,0:T(8,128)}, u32[]{:S(2)}) copy-start(f32[64,192]{1,0:T(8,128)} %get-tuple-element.11) | copy-start | bytes 147460

commit v4 on v3

--- a/solution.py
+++ b/solution.py
@@ -13,6 +13,7 @@
 CHIPS = SPLIT * SPLIT
 CAP = 16
 STEP = 512
+VMEM_BYTES = 64 * 1024 * 1024 - 131072
 PIECES = 2
 LAST = (((1,), (1,)), ((), ()))
 FIRST = (((0,), (0,)), ((), ()))
@@ -395,7 +396,7 @@
         )
         return carry
 
-    lax.fori_loop(0, chunks, project, 0)
+    lax.fori_loop(0, chunks, project, 0, unroll=True)
 
     pre_gate = pre[:, :hidden]
     pre_up = pre[:, hidden:]
@@ -415,7 +416,7 @@
         parts[:, :, :, cols] = part.astype(jnp.bfloat16).reshape(SPLIT, SPLIT, CAP, STEP)
         return carry
 
-    lax.fori_loop(0, chunks, back_project, 0)
+    lax.fori_loop(0, chunks, back_project, 0, unroll=True)
 
     def part_copy(side, place_here):
         return copy_to(
@@ -433,8 +434,11 @@
 
     lax.fori_loop(1, SPLIT + 1, send_parts, 0)
 
+    def column(i):
+        return lax.rem(x + i, SPLIT)
+
     def sibling_copy(i):
-        some = pl.ds(i * SPLIT, SPLIT)
+        some = pl.ds(column(i) * SPLIT, SPLIT)
         return copy_to(
             grads.at[1 - core, some],
             sibling_grads.at[some],
@@ -443,24 +447,60 @@
             sibling,
         )
 
-    def weight_grads(i, carry):
-        for half in range(1):
-            c = i + half
-            cols = pl.ds(pl.multiple_of(c * STEP, STEP), STEP)
-            left = rows_in[:, :, :, cols].reshape(n_rows, STEP)
-            one = lax.dot_general(left, pair[...], FIRST, preferred_element_type=jnp.float32)
-            left = rows_grad[:, :, :, cols].reshape(n_rows, STEP)
-            two = lax.dot_general(left, active[...], FIRST, preferred_element_type=jnp.float32)
-            one = one.astype(jnp.bfloat16).reshape(blocks, depth, 2 * hidden)
-            two = two.reshape(blocks, 2, depth // 2, hidden)
-            for b in range(blocks):
-                to = c * (blocks // 2) + b // 2
-                grads[b % 2, to, :depth] = one[b]
-                grads[b % 2, to, depth:] = beside(two[b, 0], two[b, 1])
+    def weight_grads(i):
+        c = column(i)
+        cols = pl.ds(pl.multiple_of(c * STEP, STEP), STEP)
+        left = rows_in[:, :, :, cols].reshape(n_rows, STEP)
+        one = lax.dot_general(left, pair[...], FIRST, preferred_element_type=jnp.float32)
+        left = rows_grad[:, :, :, cols].reshape(n_rows, STEP)
+        two = lax.dot_general(left, active[...], FIRST, preferred_element_type=jnp.float32)
+        one = one.astype(jnp.bfloat16).reshape(blocks, depth, 2 * hidden)
+        two = two.reshape(blocks, 2, depth // 2, hidden)
+        for b in range(blocks):
+            to = c * (blocks // 2) + b // 2
+            grads[b % 2, to, :depth] = one[b]
+            grads[b % 2, to, depth:] = beside(two[b, 0], two[b, 1])
         sibling_copy(i).start()
-        return carry
-
-    lax.fori_loop(0, SPLIT, weight_grads, 0)
+
+    def grad_copy(to, h):
+        return copy_to(
+            grads.at[core, to, rows_of(h)],
+            grads_in.at[chip, rows_of(h)],
+            grad_send.at[to, h],
+            grad_recv.at[chip, h],
+            (2 * to + core, z),
+        )
+
+    def send_grads(i):
+        some = sibling_grads.at[pl.ds(column(i) * SPLIT, SPLIT)]
+        copy_to(some, some, sibling_send.at[i], sibling_recv.at[i], sibling).wait_recv()
+        for step in range(SPLIT):
+            to = column(i) * SPLIT + lax.rem(y + step, SPLIT)
+            total = grads[core, to].astype(jnp.float32) + sibling_grads[to].astype(jnp.float32)
+            grads[core, to] = total.astype(jnp.bfloat16)
+            pl.when(to != chip)(grad_copy(to, 0).start)
+
+    def grads_out(i, carry):
+        weight_grads(i)
+
+        @pl.when(i > 0)
+        def _():
+            send_grads(i - 1)
+
+        return carry
+
+    def send_later(to, carry):
+        @pl.when(to != chip)
+        def _():
+            for h in range(1, PIECES):
+                grad_copy(to, h).start()
+
+        return carry
+
+    lax.fori_loop(0, SPLIT, grads_out, 0)
+    send_grads(SPLIT - 1)
+    grads_in[chip] = grads[core, chip]
+    lax.fori_loop(0, CHIPS, send_later, 0)
 
     def sum_parts(place_here):
         for side in range(3):
@@ -495,50 +535,30 @@
 
     lax.fori_loop(1, SPLIT, send_finals, 0)
 
-    def grad_copy(i, h):
-        to = lax.rem(chip + i, CHIPS)
-        return copy_to(
-            grads.at[core, to, rows_of(h)],
-            grads_in.at[chip, rows_of(h)],
-            grad_send.at[i, h],
-            grad_recv.at[chip, h],
-            (2 * to + core, z),
-        )
-
-    def sibling_arrived(i, carry):
-        some = pl.ds(i * SPLIT, SPLIT)
-        copy_to(
-            sibling_grads.at[some],
-            sibling_grads.at[some],
-            sibling_send.at[i],
-            sibling_recv.at[i],
-            sibling,
-        ).wait_recv()
-        return carry
-
-    lax.fori_loop(0, SPLIT, sibling_arrived, 0)
-
-    def chip_sum(to):
-        return (
-            grads[core, to].astype(jnp.float32) + sibling_grads[to].astype(jnp.float32)
-        ).astype(jnp.bfloat16)
-
-    grads_in[chip] = chip_sum(chip)
-
-    def send_grads(i, carry):
-        to = lax.rem(chip + i, CHIPS)
-        grads[core, to] = chip_sum(to)
-        grad_copy(i, 0).start()
-        return carry
-
-    lax.fori_loop(1, CHIPS, send_grads, 0)
-
-    def send_later(i, carry):
-        for h in range(1, PIECES):
-            grad_copy(i, h).start()
-        return carry
-
-    lax.fori_loop(1, CHIPS, send_later, 0)
+    for copy in entries:
+        copy.wait_send()
+
+    def drain_in(i, carry):
+        for h in range(PIECES):
+            for to_y in range(SPLIT):
+                elsewhere, copy = spread_copy(i, to_y, h)
+                pl.when(elsewhere)(copy.wait_send)
+        for side in range(3):
+            for h in range(2):
+                side_copy(side, i, h).wait_send()
+        return carry
+
+    lax.fori_loop(0, SPLIT, drain_in, 0)
+
+    def drain_twins(i, carry):
+        for h in range(PIECES):
+            twin_copy(i, h).wait_send()
+        return carry
+
+    lax.fori_loop(0, CHIPS, drain_twins, 0)
+    for h in range(PIECES):
+        for i in range(1, SPLIT):
+            shard_copy(i, h).wait_send()
 
     sum_parts(0)
 
@@ -601,6 +621,23 @@
         return carry
 
     lax.fori_loop(0, 3 * PIECES, send_group, 0)
+
+    def drain_out(i, carry):
+        for side in range(3):
+            part_copy(side, i).wait_send()
+        sibling_copy(i).wait_send()
+        return carry
+
+    def drain_grads(i, carry):
+        for h in range(PIECES):
+            grad_copy(lax.rem(chip + i, CHIPS), h).wait_send()
+        return carry
+
+    lax.fori_loop(0, SPLIT, drain_out, 0)
+    for i in range(1, SPLIT):
+        final_copy(i).wait_send()
+    lax.fori_loop(1, CHIPS, drain_grads, 0)
+
     total = jnp.concatenate([plane_sum(member, h) for h in range(PIECES)], axis=0)
     for i in range(1, SPLIT):
         for h in range(PIECES):
@@ -612,46 +649,22 @@
     grad_down[: depth // 2] = total[depth:, :hidden]
     grad_down[depth // 2 :] = total[depth:, hidden:]
 
-    for copy in entries:
-        copy.wait_send()
-
-    def drain_places(place_here, carry):
-        for side in range(3):
-            part_copy(side, place_here).wait_send()
-            for h in range(2):
-                side_copy(side, place_here, h).wait_send()
-        return carry
-
-    lax.fori_loop(0, SPLIT, drain_places, 0)
-
-    def drain_spread(part, carry):
-        for to_y in range(SPLIT):
-            for h in range(PIECES):
-                elsewhere, copy = spread_copy(part, to_y, h)
-                pl.when(elsewhere)(copy.wait_send)
-        sibling_copy(part).wait_send()
-        return carry
-
-    lax.fori_loop(0, SPLIT, drain_spread, 0)
-
-    def drain_some(i, carry):
-        final_copy(i).wait_send()
-        for h in range(PIECES):
-            shard_copy(i, h).wait_send()
+    for h in range(PIECES):
+        for i in range(1, SPLIT):
             group_copy(i, h).wait_send()
-        return carry
-
-    lax.fori_loop(1, SPLIT, drain_some, 0)
-    for h in range(PIECES):
-        twin_copy(0, h).wait_send()
-
-    def drain_chips(i, carry):
-        for h in range(PIECES):
-            twin_copy(i, h).wait_send()
-            grad_copy(i, h).wait_send()
-        return carry
-
-    lax.fori_loop(1, CHIPS, drain_chips, 0)
+
+
+def hand_over(*refs):
+    sources, targets, held = refs[:4], refs[4:8], refs[8:12]
+    reads = [pltpu.make_async_copy(sources[i], held[i], refs[12].at[i]) for i in range(4)]
+    writes = [pltpu.make_async_copy(held[i], targets[i], refs[13].at[i]) for i in range(4)]
+    for copy in reads:
+        copy.start()
+    for read, write in zip(reads, writes):
+        read.wait()
+        write.start()
+    for copy in writes:
+        copy.wait()
 
 
 def body(tokens, cotangent, ids, mask, gates, gate_w, up_w, down_w):
@@ -725,12 +738,22 @@
             dma((SPLIT, PIECES)),
         ],
         compiler_params=pltpu.CompilerParams(
-            collective_id=0, has_side_effects=True, vmem_limit_bytes=64 * 1024 * 1024 - 131072
+            collective_id=0, has_side_effects=True, vmem_limit_bytes=VMEM_BYTES
         ),
         cost_estimate=pl.CostEstimate(
             flops=16 * n_rows * width * hidden, bytes_accessed=1 << 21, transcendentals=1 << 16
         ),
     )(tokens, cotangent, ids.T, mask.T, gates.T, gate_w, up_w, down_w.T)
+    anywhere = pl.BlockSpec(memory_space=pl.ANY)
+    results = (grad_tokens, grad_gate, grad_up, grad_down)
+    grad_tokens, grad_gate, grad_up, grad_down = pl.pallas_call(
+        hand_over,
+        out_shape=tuple(jax.ShapeDtypeStruct(r.shape, r.dtype) for r in results),
+        in_specs=[anywhere] * 4,
+        out_specs=[anywhere] * 4,
+        scratch_shapes=[pltpu.VMEM(r.shape, r.dtype) for r in results] + [dma((4,)), dma((4,))],
+        compiler_params=pltpu.CompilerParams(vmem_limit_bytes=VMEM_BYTES),
+    )(*results)
     return grad_tokens, grad_gate, grad_up, grad_down.T
 
 

time: 84.6 us -> 80.4 us (0.950)
  local copies, waits for them, and re-layouts: 4.27 us -> 0 us
    unnamed x10 -> x0, local copies, waits for them, and re-layouts: 4.27 us -> none
    pallas_call x1, Pallas kernels: 79.4 us -> 77.3 us  [body(): pl.pallas_call(kernel, out_shape=(jax.ShapeDtypeStruct((n_tok, width), bf...]
    pallas_call x0 -> x1, Pallas kernels: none -> 1.96 us  [body(): pl.pallas_call(hand_over, out_shape=tuple((jax.ShapeDtypeStruct(r.shape,...]
where the time goes in v4:
time: 80.4 us; the launch traced here: 79.8 us
  Pallas kernels  79.2 us (99%)
    pallas_call x1, Pallas kernels, body(): pl.pallas_call(kernel, out_shape=(jax.ShapeDtypeStruct((n_tok, width), bf...  77.3 us
    pallas_call x1, Pallas kernels, body(): pl.pallas_call(hand_over, out_shape=tuple((jax.ShapeDtypeStruct(r.shape,...  1.96 us

profile of v4, /device:TPU:24, one launch (start us, length us, event | category | flops | bytes accessed | tf_op | source)
XLA Modules:
  0.0 79.8 jit_solution(2470597043117107320)
XLA Ops:
  0.6 77.3 %shard_map.111 = (bf16[128,2048]{1,0:T(8,128)(2,1)}, f32[64,192]{1,0:T(8,128)}, f32[64,192]{1,0:T(8,128)}, f32[64,192]{1,0:T(8,128)}) custom-call(bf16[128,2048]{1,0:T(8,128)(2,1)} %tokens_hbm.1, bf16[128,2048]{1,0:T(8,128)(2,1)} %cotangent_hbm.1, s32[8,128]{1,0:T(8,128)} %bitcast.7, s32[8,128]{1,0:T(8,128)} %bitcast.8, f32[8,128]{1,0:T(8,128)} %bitcast.9, ...), custom_call_target="tpu_custom_call" | custom-call | flops 1610612736 | bytes 2097152 | tf_op jit(solution)/shard_map/pallas_call | solution.py:679
  77.9 2.0 %shard_map.112 = (bf16[128,2048]{1,0:T(8,128)(2,1)}, f32[64,192]{1,0:T(8,128)}, f32[64,192]{1,0:T(8,128)}, f32[64,192]{1,0:T(8,128)}) custom-call(bf16[128,2048]{1,0:T(8,128)(2,1)} %get-tuple-element.12.refs_0_, f32[64,192]{1,0:T(8,128)} %get-tuple-element.13.refs_1_, f32[64,192]{1,0:T(8,128)} %get-tuple-element.14.refs_2_, f32[64,192]{1,0:T(8,128)} %get-tuple-element.15.refs_3_), custom_call_target="tpu_custom_call" | custom-call | tf_op jit(solution)/shard_map/pallas_call | solution.py:749

commit v5 on v4

--- a/solution.py
+++ b/solution.py
@@ -157,8 +157,8 @@
         )
         return carry
 
-    lax.fori_loop(1, RING, greet_ring, 0)
-    lax.fori_loop(1, CHIPS, greet_plane, 0)
+    lax.fori_loop(1, RING, greet_ring, 0, unroll=True)
+    lax.fori_loop(1, CHIPS, greet_plane, 0, unroll=True)
     pl.semaphore_signal(barrier, inc=1, device_id=sibling, device_id_type=MESH)
 
     for load in loads[:3]:
@@ -206,7 +206,7 @@
         )
         return carry
 
-    lax.fori_loop(0, chunks, fill, 0)
+    lax.fori_loop(0, chunks, fill, 0, unroll=True)
     rows_in[0, 0] = out_in[group]
     rows_grad[0, 0] = out_grad[group]
 
@@ -427,12 +427,17 @@
             from_sides[side],
         )
 
+    def far_first(i):
+        return (1 - edge) * i + edge * (1 + lax.rem(i, 3))
+
     def send_parts(i, carry):
         for side in range(3):
-            part_copy(side, lax.rem(i, SPLIT)).start()
-        return carry
-
-    lax.fori_loop(1, SPLIT + 1, send_parts, 0)
+            part_copy(side, far_first(i)).start()
+        return carry
+
+    lax.fori_loop(1, SPLIT, send_parts, 0)
+    for side in range(3):
+        part_copy(side, 0).start()
 
     def column(i):
         return lax.rem(x + i, SPLIT)
@@ -528,7 +533,8 @@
             plane((2 * upper - 1) * distance),
         )
 
-    def send_finals(place_here, carry):
+    def send_finals(i, carry):
+        place_here = far_first(i)
         sum_parts(place_here)
         final_copy(place_here).start()
         return carry
@@ -589,7 +595,7 @@
         ).astype(jnp.bfloat16)
         return carry
 
-    lax.fori_loop(0, chunks, give_back, 0)
+    lax.fori_loop(0, chunks, give_back, 0, unroll=True)
 
     def plane_sum(part, h):
         total = jnp.zeros((piece, 2 * hidden), jnp.float32)

time: 80.4 us -> 81.7 us (1.016)
  Pallas kernels: 79.2 us -> 80.2 us
    pallas_call x1, Pallas kernels: 77.3 us -> 78.2 us  [body(): pl.pallas_call(kernel, out_shape=(jax.ShapeDtypeStruct((n_tok, width), bf...]
where the time goes in v5:
time: 81.7 us; the launch traced here: 80.8 us
  Pallas kernels  80.2 us (98%)
    pallas_call x1, Pallas kernels, body(): pl.pallas_call(kernel, out_shape=(jax.ShapeDtypeStruct((n_tok, width), bf...  78.2 us
    pallas_call x1, Pallas kernels, body(): pl.pallas_call(hand_over, out_shape=tuple((jax.ShapeDtypeStruct(r.shape,...  1.96 us

profile of v5, /device:TPU:24, one launch (start us, length us, event | category | flops | bytes accessed | tf_op | source)
XLA Modules:
  0.0 80.8 jit_solution(8755371327873826027)
XLA Ops:
  0.6 78.2 %shard_map.111 = (bf16[128,2048]{1,0:T(8,128)(2,1)}, f32[64,192]{1,0:T(8,128)}, f32[64,192]{1,0:T(8,128)}, f32[64,192]{1,0:T(8,128)}) custom-call(bf16[128,2048]{1,0:T(8,128)(2,1)} %tokens_hbm.1, bf16[128,2048]{1,0:T(8,128)(2,1)} %cotangent_hbm.1, s32[8,128]{1,0:T(8,128)} %bitcast.7, s32[8,128]{1,0:T(8,128)} %bitcast.8, f32[8,128]{1,0:T(8,128)} %bitcast.9, ...), custom_call_target="tpu_custom_call" | custom-call | flops 1610612736 | bytes 2097152 | tf_op jit(solution)/shard_map/pallas_call | solution.py:685
  78.8 2.0 %shard_map.112 = (bf16[128,2048]{1,0:T(8,128)(2,1)}, f32[64,192]{1,0:T(8,128)}, f32[64,192]{1,0:T(8,128)}, f32[64,192]{1,0:T(8,128)}) custom-call(bf16[128,2048]{1,0:T(8,128)(2,1)} %get-tuple-element.12.refs_0_, f32[64,192]{1,0:T(8,128)} %get-tuple-element.13.refs_1_, f32[64,192]{1,0:T(8,128)} %get-tuple-element.14.refs_2_, f32[64,192]{1,0:T(8,128)} %get-tuple-element.15.refs_3_), custom_call_target="tpu_custom_call" | custom-call | tf_op jit(solution)/shard_map/pallas_call | solution.py:755
